TPU v7x, 512 devices: a whole 4x4x16 slice. The times are simulated.
512 devices in a mesh: pair: 128 (over x, z, core), aux: 4 (over y).
Axes of the slice: x: 4, y: 4, z: 16, core: 2. Of those that a mesh axis runs over, the one named last changes fastest.
Arguments:
- integrals: bfloat16 [8192, 256, 256], P('pair', 'aux'), may hold values from -4 to 4
- amplitudes: bfloat16 [8192, 128, 128], P(('pair', 'aux')), may hold values from -4 to 4
- coeffs: bfloat16 [8192, 128, 128], P(('pair', 'aux')), may hold values from -0.5 to 0.5
- domains: int32 [8192, 128], P(('pair', 'aux')), may hold values from 0 to 4247, as said below
- neighbours: int32 [8192, 8], P(('pair', 'aux')), may hold values from 0 to 8191, as said below
- counts: int32 [8192], P(('pair', 'aux')), may hold values from 1 to 8, as said below
- couplings: float32 [8192, 8], P(('pair', 'aux')), may hold values from -1 to 1
- pno_energies: float32 [8192, 128], P(('pair', 'aux')), may hold values from 0.3 to 3
- occ_energies: float32 [8192], P(('pair', 'aux')), may hold values from 1 to 4
Outputs:
- residual: float32 [8192, 128, 128], P(('pair', 'aux'))
- updated_amplitudes: bfloat16 [8192, 128, 128], P(('pair', 'aux'))
Inputs may be any that keep to these rules, and one draw needn't show every extreme that they name: `domains`: each row holds 128 distinct PAO numbers in rising order. `neighbours`: pairs are numbered device by device along pair+aux, 16 a device; every slot of pair p names a pair whose device differs from p's device by at most 1. Only the first counts[p] slots of pair p are active.
All inputs are finite; a program needn't handle non-finite values.
Results may differ from a plain program's by a relative error of at most 0.0034.
Values may be sent and summed in bfloat16 or wider, within the bound.
A program may use at most 128 MiB of HBM per device.

v0:
```python
import jax
import jax.numpy as jnp
from jax import lax
from jax.sharding import PartitionSpec as P

REACH = 1


def with_halo(cells, sides, width):
    for axis, dim in sides:
        count = lax.axis_size(axis)
        ends = count - 1
        head = lax.slice_in_dim(cells, 0, width, axis=dim)
        tail = lax.slice_in_dim(cells, cells.shape[dim] - width, cells.shape[dim], axis=dim)
        cells = jnp.concatenate(
            [
                lax.ppermute(tail, axis, [(i, (i + 1) % count) for i in range(ends)]),
                cells,
                lax.ppermute(head, axis, [((i + 1) % count, i) for i in range(ends)]),
            ],
            axis=dim,
        )
    return cells


def pno_to_pao(amplitudes, coeffs):
    left_half = jnp.einsum(
        "pdn,pnm->pdm", coeffs, amplitudes, preferred_element_type=jnp.float32
    ).astype(jnp.bfloat16)
    return jnp.einsum("pdm,pem->pde", left_half, coeffs, preferred_element_type=jnp.float32).astype(
        jnp.bfloat16
    )


def per_device(
    integrals,
    amplitudes,
    coeffs,
    domains,
    neighbours,
    counts,
    couplings,
    pno_energies,
    occ_energies,
):
    pairs_here = amplitudes.shape[0]
    width_pno = amplitudes.shape[1]
    regrouped = lax.all_to_all(integrals, "aux", split_axis=0, concat_axis=1, tiled=True)
    exchange_part = jnp.einsum(
        "pqa,pqb->pab",
        regrouped[:, :, :width_pno],
        regrouped[:, :, width_pno:],
        preferred_element_type=jnp.float32,
    )
    reach_rows = REACH * pairs_here
    ext_amps, ext_coeffs, ext_domains = (
        with_halo(amplitudes, ((("pair", "aux"), 0),), reach_rows),
        with_halo(coeffs, ((("pair", "aux"), 0),), reach_rows),
        with_halo(domains, ((("pair", "aux"), 0),), reach_rows),
    )
    pao_amps = pno_to_pao(ext_amps, ext_coeffs)
    first_row = (lax.axis_index(("pair", "aux")) - REACH) * pairs_here
    local_rows = neighbours - first_row
    far_amps = pao_amps[local_rows]
    far_domains = ext_domains[local_rows]
    matches = (domains[:, None, :, None] == far_domains[:, :, None, :]).astype(jnp.bfloat16)
    select = jnp.einsum(
        "pan,pkab->pknb", coeffs, matches, preferred_element_type=jnp.float32
    ).astype(jnp.bfloat16)
    half_done = jnp.einsum(
        "pknb,pkbe->pkne", select, far_amps, preferred_element_type=jnp.float32
    ).astype(jnp.bfloat16)
    projected = jnp.einsum("pkne,pkme->pknm", half_done, select, preferred_element_type=jnp.float32)
    slots = lax.broadcasted_iota(jnp.int32, couplings.shape, 1)
    weights = jnp.where(slots < counts[:, None], couplings, jnp.zeros_like(couplings))
    coupled = jnp.einsum("pk,pknm->pnm", weights, projected, precision=lax.Precision.HIGHEST)
    denominator = pno_energies[:, :, None] + pno_energies[:, None, :] + occ_energies[:, None, None]
    amps_wide = amplitudes.astype(jnp.float32)
    residual = exchange_part + denominator * amps_wide + coupled
    updated = (amps_wide - residual / denominator).astype(jnp.bfloat16)
    return (residual, updated)


def solution(mesh):
    in_specs = (
        P("pair", "aux", None),
        P(("pair", "aux"), None, None),
        P(("pair", "aux"), None, None),
        P(("pair", "aux"), None),
        P(("pair", "aux"), None),
        P(("pair", "aux")),
        P(("pair", "aux"), None),
        P(("pair", "aux"), None),
        P(("pair", "aux")),
    )
    out_specs = (P(("pair", "aux"), None, None), P(("pair", "aux"), None, None))
    return jax.shard_map(
        per_device, mesh=mesh, in_specs=in_specs, out_specs=out_specs, check_vma=False
    )
```

profile of v0, /device:TPU:485, one launch (start us, length us, event | category | flops | bytes accessed | tf_op | source)
XLA Modules:
  0.0 100.7 jit_solution(13905877611827954037)
XLA Ops:
  0.7 3.3 %collective-permute-start.2 = (bf16[16,128,128]{2,1,0:T(8,128)(2,1)}, bf16[16,128,128]{2,1,0:T(8,128)(2,1)S(1)}, u32[]{:S(2)}, u32[]{:S(2)}) collective-permute-start(bf16[16,128,128]{2,1,0:T(8,128)(2,1)} %param.11), channel_id=1, source_target_pairs={{0,1},{1,2},{2,3},{3,4},{4,5},{5,6},{6,7},{7,8},{8,9},{9,10},{10,1... | collective-permute-start | bytes 1572872 | tf_op jit(solution)/shard_map/ppermute | solution.py:17
  4.0 3.9 %collective-permute-start.3 = (bf16[16,128,128]{2,1,0:T(8,128)(2,1)}, bf16[16,128,128]{2,1,0:T(8,128)(2,1)S(1)}, u32[]{:S(2)}, u32[]{:S(2)}) collective-permute-start(bf16[16,128,128]{2,1,0:T(8,128)(2,1)} %param.11), channel_id=1, source_target_pairs={{1,0},{2,1},{3,2},{4,3},{5,4},{6,5},{7,6},{8,7},{9,8},{10,9},{11,1... | collective-permute-start | bytes 1572872 | tf_op jit(solution)/shard_map/ppermute | solution.py:19
  8.0 1.9 %collective-permute-start = (s32[16,128]{1,0:T(8,128)}, s32[16,128]{1,0:T(8,128)S(1)}, u32[]{:S(2)}, u32[]{:S(2)}) collective-permute-start(s32[16,128]{1,0:T(8,128)} %param.12), channel_id=1, source_target_pairs={{0,1},{1,2},{2,3},{3,4},{4,5},{5,6},{6,7},{7,8},{8,9},{9,10},{10,1... | collective-permute-start | bytes 24584 | tf_op jit(solution)/shard_map/ppermute | solution.py:17
  9.9 4.9 %collective-permute-start.1 = (s32[16,128]{1,0:T(8,128)}, s32[16,128]{1,0:T(8,128)S(1)}, u32[]{:S(2)}, u32[]{:S(2)}) collective-permute-start(s32[16,128]{1,0:T(8,128)} %param.12), channel_id=1, source_target_pairs={{1,0},{2,1},{3,2},{4,3},{5,4},{6,5},{7,6},{8,7},{9,8},{10,9},{11,1... | collective-permute-start | bytes 24584 | tf_op jit(solution)/shard_map/ppermute | solution.py:19
  14.7 1.9 %collective-permute-start.4 = (bf16[16,128,128]{2,1,0:T(8,128)(2,1)}, bf16[16,128,128]{2,1,0:T(8,128)(2,1)}, u32[]{:S(2)}, u32[]{:S(2)}) collective-permute-start(bf16[16,128,128]{2,1,0:T(8,128)(2,1)} %param.10), channel_id=1, source_target_pairs={{0,1},{1,2},{2,3},{3,4},{4,5},{5,6},{6,7},{7,8},{8,9},{9,10},{10,1... | collective-permute-start | bytes 1572872 | tf_op jit(solution)/shard_map/ppermute | solution.py:17
  16.7 9.7 %all-to-all-start = ((bf16[64,64,256]{2,1,0:T(8,128)(2,1)}), bf16[64,64,256]{2,1,0:T(8,128)(2,1)}, u32[]{:S(2)}, u32[]{:S(2)}) async-start(bf16[64,64,256]{2,1,0:T(8,128)(2,1)} %param.9), calls=%async_computation | async-start | bytes 4194304 | tf_op jit(solution)/shard_map/all_to_all | solution.py:48
  26.4 0.1 copy.16
  26.4 0.1 reshape.12
  26.6 0.1 copy.19
  26.6 0.0 collective-permute-done
  26.6 1.9 %collective-permute-start.5 = (bf16[16,128,128]{2,1,0:T(8,128)(2,1)}, bf16[16,128,128]{2,1,0:T(8,128)(2,1)}, u32[]{:S(2)}, u32[]{:S(2)}) collective-permute-start(bf16[16,128,128]{2,1,0:T(8,128)(2,1)} %param.10), channel_id=1, source_target_pairs={{1,0},{2,1},{3,2},{4,3},{5,4},{6,5},{7,6},{8,7},{9,8},{10,9},{11,1... | collective-permute-start | bytes 1572872 | tf_op jit(solution)/shard_map/ppermute | solution.py:19
  28.6 0.6 gather_fusion
  29.3 5.5 %fusion.2 = bf16[16,8,128,128]{3,2,1,0:T(8,128)(2,1)} fusion(s32[16,8,128]{2,1,0:T(8,128)S(1)} %bitcast.24, s32[16,128]{1,0:T(8,128)S(1)} %copy-done.1, bf16[16,128,128]{2,1,0:T(8,128)(2,1)S(1)} %copy-done), kind=kOutput, calls=%fused_computation.4 | convolution fusion | flops 538968064 | bytes 4792320 | tf_op jit(solution)/shard_map/pan,pkab->pknb/dot_general | solution.py:67
  34.8 0.1 constant_dynamic-update-slice_fusion.1
  34.9 0.1 constant_dynamic-update-slice_fusion
  35.0 29.0 %collective-permute-done.5 = bf16[16,128,128]{2,1,0:T(8,128)(2,1)} collective-permute-done((bf16[16,128,128]{2,1,0:T(8,128)(2,1)}, bf16[16,128,128]{2,1,0:T(8,128)(2,1)}, u32[]{:S(2)}, u32[]{:S(2)}) %collective-permute-start.5) | collective-permute-done | bytes 524320 | tf_op jit(solution)/shard_map/ppermute | solution.py:19
  64.0 3.1 %convolution_convert_fusion = bf16[48,128,128]{2,1,0:T(8,128)(2,1)S(1)} fusion(bf16[48,128,128]{2,1,0:T(8,128)(2,1)S(1)} %constant_dynamic-update-slice_fusion, bf16[16,128,128]{2,1,0:T(8,128)(2,1)} %collective-permute-done.5, bf16[16,128,128]{2,1,0:T(8,128)(2,1)} %param.10, bf16[16,128,128]{2,1,0:T(8,128)(2,1)} %collective-permute-done.4), kind=kOutput, calls=%fused_computation.12 | convolution fusion | flops 405798912 | bytes 4718592 | tf_op jit(solution)/shard_map/pdm,pem->pde/dot_general | solution.py:30
  67.1 3.0 %gather_fusion.1 = bf16[128,128,128]{2,1,0:T(8,128)(2,1)} fusion(bf16[48,128,128]{2,1,0:T(8,128)(2,1)S(1)} %convolution_convert_fusion, s32[1024]{0:T(1024)S(1)} %pad_clamp_fusion), kind=kCustom, calls=%fused_computation.1 | custom fusion | bytes 8389120 | tf_op jit(solution)/shard_map/gather | solution.py:64
  70.1 10.5 %fusion.4 = f32[16,8,128,128]{3,2,1,0:T(8,128)} fusion(bf16[16,8,128,128]{3,2,1,0:T(8,128)(2,1)} %bitcast.21, bf16[16,8,128,128]{3,2,1,0:T(8,128)(2,1)} %fusion.2), kind=kOutput, calls=%fused_computation.6 | convolution fusion | flops 1075838976 | bytes 16777216 | tf_op jit(solution)/shard_map/pkne,pkme->pknm/dot_general | solution.py:73
  80.6 15.3 %fusion = f32[16,1,128,128]{3,1,2,0:T(1,128)S(1)} fusion(f32[16,8,1,1]{1,2,3,0:T(1,128)S(1)} %copy.19, f32[16,8,128,128]{3,2,1,0:T(8,128)} %fusion.4), kind=kOutput, calls=%fused_computation.2 | convolution fusion | flops 25165824 | bytes 9437696 | tf_op jit(solution)/shard_map/pk,pknm->pnm/dot_general | solution.py:76
  95.9 0.0 copy-start.5
  95.9 0.0 copy-start.6
  95.9 1.7 %copy.14 = bf16[4,16,64,256]{3,2,0,1:T(8,128)(2,1)S(1)} copy(bf16[4,16,64,256]{3,2,1,0:T(8,128)(2,1)} %bitcast) | data formatting | bytes 4194304 | tf_op jit(solution)/shard_map/all_to_all | solution.py:48
  97.7 3.0 %fusion.20 = (bf16[16,128,128]{2,1,0:T(8,128)(2,1)}, f32[16,128,128]{2,1,0:T(8,128)}) fusion(bf16[16,128,128]{2,1,0:T(8,128)(2,1)} %param.10, f32[16]{0:T(128)S(1)} %copy-done.6, f32[16,128]{1,0:T(8,128)S(1)} %copy-done.5, f32[16,128,128]{2,1,0:T(8,128)S(1)} %bitcast.23, bf16[16,256,256]{2,1,0:T(8,128)(2,1)S(1)} %bitcast.22), kind=kOutput, calls=%fused_computation.23 | convolution fusion | flops 136577024 | bytes 5259776 | tf_op jit(solution)/shard_map/pqa,pqb->pab/dot_general | solution.py:49
  (22 shorter events, 0.1 us)
Async XLA Ops:
  0.6 28.6 %copy-start = (bf16[16,128,128]{2,1,0:T(8,128)(2,1)S(1)}, bf16[16,128,128]{2,1,0:T(8,128)(2,1)}, u32[]{:S(2)}) copy-start(bf16[16,128,128]{2,1,0:T(8,128)(2,1)} %param.11) | copy-start | bytes 1572868
  0.6 27.9 %copy-start.1 = (s32[16,128]{1,0:T(8,128)S(1)}, s32[16,128]{1,0:T(8,128)}, u32[]{:S(2)}) copy-start(s32[16,128]{1,0:T(8,128)} %param.12) | copy-start | bytes 24580
  0.7 25.7 %copy-start.2 = (s32[16,8]{0,1:T(8,128)S(1)}, s32[16,8]{0,1:T(8,128)}, u32[]{:S(2)}) copy-start(s32[16,8]{0,1:T(8,128)} %param.13) | copy-start | bytes 1540
  0.7 25.9 %copy-start.4 = (s32[16]{0:T(128)S(1)}, s32[16]{0:T(128)}, u32[]{:S(2)}) copy-start(s32[16]{0:T(128)} %param.14) | copy-start | bytes 196
  0.7 25.9 %copy-start.3 = (f32[16,8]{0,1:T(8,128)S(1)}, f32[16,8]{0,1:T(8,128)}, u32[]{:S(2)}) copy-start(f32[16,8]{0,1:T(8,128)} %param.15) | copy-start | bytes 1540
  0.7 34.1 %collective-permute-start.2 = (bf16[16,128,128]{2,1,0:T(8,128)(2,1)}, bf16[16,128,128]{2,1,0:T(8,128)(2,1)S(1)}, u32[]{:S(2)}, u32[]{:S(2)}) collective-permute-start(bf16[16,128,128]{2,1,0:T(8,128)(2,1)} %param.11), channel_id=1, source_target_pairs={{0,1},{1,2},{2,3},{3,4},{4,5},{5,6},{6,7},{7,8},{8,9},{9,10},{10,1... | collective-permute-start | bytes 1572872 | tf_op jit(solution)/shard_map/ppermute | solution.py:17
  4.0 30.9 %collective-permute-start.3 = (bf16[16,128,128]{2,1,0:T(8,128)(2,1)}, bf16[16,128,128]{2,1,0:T(8,128)(2,1)S(1)}, u32[]{:S(2)}, u32[]{:S(2)}) collective-permute-start(bf16[16,128,128]{2,1,0:T(8,128)(2,1)} %param.11), channel_id=1, source_target_pairs={{1,0},{2,1},{3,2},{4,3},{5,4},{6,5},{7,6},{8,7},{9,8},{10,9},{11,1... | collective-permute-start | bytes 1572872 | tf_op jit(solution)/shard_map/ppermute | solution.py:19
  8.0 18.7 %collective-permute-start = (s32[16,128]{1,0:T(8,128)}, s32[16,128]{1,0:T(8,128)S(1)}, u32[]{:S(2)}, u32[]{:S(2)}) collective-permute-start(s32[16,128]{1,0:T(8,128)} %param.12), channel_id=1, source_target_pairs={{0,1},{1,2},{2,3},{3,4},{4,5},{5,6},{6,7},{7,8},{8,9},{9,10},{10,1... | collective-permute-start | bytes 24584 | tf_op jit(solution)/shard_map/ppermute | solution.py:17
  9.9 18.7 %collective-permute-start.1 = (s32[16,128]{1,0:T(8,128)}, s32[16,128]{1,0:T(8,128)S(1)}, u32[]{:S(2)}, u32[]{:S(2)}) collective-permute-start(s32[16,128]{1,0:T(8,128)} %param.12), channel_id=1, source_target_pairs={{1,0},{2,1},{3,2},{4,3},{5,4},{6,5},{7,6},{8,7},{9,8},{10,9},{11,1... | collective-permute-start | bytes 24584 | tf_op jit(solution)/shard_map/ppermute | solution.py:19
  14.7 20.3 %collective-permute-start.4 = (bf16[16,128,128]{2,1,0:T(8,128)(2,1)}, bf16[16,128,128]{2,1,0:T(8,128)(2,1)}, u32[]{:S(2)}, u32[]{:S(2)}) collective-permute-start(bf16[16,128,128]{2,1,0:T(8,128)(2,1)} %param.10), channel_id=1, source_target_pairs={{0,1},{1,2},{2,3},{3,4},{4,5},{5,6},{6,7},{7,8},{8,9},{9,10},{10,1... | collective-permute-start | bytes 1572872 | tf_op jit(solution)/shard_map/ppermute | solution.py:17
  16.7 79.2 %all-to-all-start = ((bf16[64,64,256]{2,1,0:T(8,128)(2,1)}), bf16[64,64,256]{2,1,0:T(8,128)(2,1)}, u32[]{:S(2)}, u32[]{:S(2)}) async-start(bf16[64,64,256]{2,1,0:T(8,128)(2,1)} %param.9), calls=%async_computation | async-start | bytes 4194304 | tf_op jit(solution)/shard_map/all_to_all | solution.py:48
  26.6 37.4 %collective-permute-start.5 = (bf16[16,128,128]{2,1,0:T(8,128)(2,1)}, bf16[16,128,128]{2,1,0:T(8,128)(2,1)}, u32[]{:S(2)}, u32[]{:S(2)}) collective-permute-start(bf16[16,128,128]{2,1,0:T(8,128)(2,1)} %param.10), channel_id=1, source_target_pairs={{1,0},{2,1},{3,2},{4,3},{5,4},{6,5},{7,6},{8,7},{9,8},{10,9},{11,1... | collective-permute-start | bytes 1572872 | tf_op jit(solution)/shard_map/ppermute | solution.py:19
  95.9 1.8 %copy-start.5 = (f32[16,128]{1,0:T(8,128)S(1)}, f32[16,128]{1,0:T(8,128)}, u32[]{:S(2)}) copy-start(f32[16,128]{1,0:T(8,128)} %param.16) | copy-start | bytes 24580
  95.9 1.8 %copy-start.6 = (f32[16]{0:T(128)S(1)}, f32[16]{0:T(128)}, u32[]{:S(2)}) copy-start(f32[16]{0:T(128)} %param.17) | copy-start | bytes 196
where the time goes:
time: 101 us
  matrix products  37.4 us (37%)
  waiting for transfers between devices  29 us (29%)
  starting transfers between devices  27.5 us (27%)
  local copies, waits for them, and re-layouts  5.84 us (6%)
    ppermute x3, waiting for transfers between devices, with_halo(): lax.ppermute(head, axis, [((i + 1) % count, i) for i in range(ends)])  29 us
    dot_general x1, matrix products, per_device(): jnp.einsum('pk,pknm->pnm', weights, projected, precision=lax.Precision.HI...  15.3 us
    ppermute x3, starting transfers between devices, with_halo(): lax.ppermute(head, axis, [((i + 1) % count, i) for i in range(ends)])  10.7 us
    dot_general x1, matrix products, per_device(): jnp.einsum('pkne,pkme->pknm', half_done, select, preferred_element_type=j...  10.5 us
    all_to_all x1, starting transfers between devices, per_device(): lax.all_to_all(integrals, 'aux', split_axis=0, concat_axis=1, tiled=True)  9.68 us
    ppermute x3, starting transfers between devices, with_halo(): lax.ppermute(tail, axis, [(i, (i + 1) % count) for i in range(ends)])  7.18 us
    dot_general x1, matrix products, per_device(): jnp.einsum('pan,pkab->pknb', coeffs, matches, preferred_element_type=jnp....  5.54 us
    dot_general x1, matrix products, pno_to_pao(): jnp.einsum('pdm,pem->pde', left_half, coeffs, preferred_element_type=jnp....  3.08 us
  transfers between devices with their start and end apart: 7, of which 1 were waited for; matrix products, arithmetic and copies ran while one was open for 38% of the time, Pallas kernels for 0%

commit v1 on v0

v1 whole, which is shorter than its diff:
```python
import jax
import jax.numpy as jnp
from jax import lax
from jax.experimental import pallas as pl
from jax.experimental.pallas import tpu as pltpu
from jax.sharding import PartitionSpec as P

MESH = pl.DeviceIdType.MESH
F32 = jnp.float32
BF16 = jnp.bfloat16
CHUNK = 4


def contract(a, b, dim_a, dim_b):
    return lax.dot_general(a, b, (((dim_a,), (dim_b,)), ((), ())), preferred_element_type=F32)


def kernel(
    ints, amps_in, coeffs_in, domains_in, neighbours, counts, couplings,
    out,
    amps, coeffs, pao, doms, own, via, summed, arrived, acc,
    load_sem, own_sem, via_sem, raw_send, raw_recv, near_send, near_recv,
    summed_send, summed_recv, halo_send, halo_recv, dom_send, dom_recv, out_sem,
):
    n_pair, n_aux = lax.axis_size("pair"), lax.axis_size("aux")
    pair, aux = lax.axis_index("pair"), lax.axis_index("aux")
    pairs = amps.shape[0]
    half = pairs // 2
    depth = ints.shape[1]
    width = amps.shape[1]
    slots = neighbours.shape[0]
    chunks = half // CHUNK

    up, down, far = (aux + 1) % n_aux, (aux + n_aux - 1) % n_aux, (aux + 2) % n_aux
    to_up, to_down = (pair, up), (pair, down)
    to_right = ((pair + (aux + 1) // n_aux) % n_pair, up)
    to_left = ((pair + n_pair - (n_aux - aux) // n_aux) % n_pair, down)

    barrier = pltpu.get_barrier_semaphore()
    for device in (to_up, to_down, to_right, to_left):
        pl.semaphore_signal(barrier, inc=1, device_id=device, device_id_type=MESH)

    def remote(src, dst, send, recv, device):
        return pltpu.make_async_remote_copy(
            src_ref=src, dst_ref=dst, send_sem=send, recv_sem=recv, device_id=device, device_id_type=MESH
        )

    def rows(first, count=CHUNK):
        return pl.ds(first, count)

    loads = [
        pltpu.make_async_copy(coeffs_in, coeffs, load_sem.at[0]),
        pltpu.make_async_copy(amps_in, amps, load_sem.at[1]),
        pltpu.make_async_copy(domains_in, doms.at[rows(pairs, pairs)], load_sem.at[2]),
    ]
    via_loads = [
        pltpu.make_async_copy(
            ints.at[rows(down * pairs, half)], via.at[0, :, pl.ds(0, depth)], via_sem.at[0]
        ),
        pltpu.make_async_copy(
            ints.at[rows(up * pairs + half, half)], via.at[1, :, pl.ds(0, depth)], via_sem.at[1]
        ),
    ]
    own_load = pltpu.make_async_copy(ints.at[rows(aux * pairs, pairs)], own.at[:, pl.ds(0, depth)], own_sem)
    for copy in loads + via_loads + [own_load]:
        copy.start()

    for copy in loads:
        copy.wait()

    def to_pao(p, carry):
        c = coeffs[p]
        left_half = contract(c, amps[p], 1, 0).astype(BF16)
        pao[pairs + p] = contract(left_half, c, 1, 1).astype(BF16)
        return carry

    lax.fori_loop(0, pairs, to_pao, 0)

    pl.semaphore_wait(barrier, 4)

    raw = []
    for c in range(chunks):
        for side, device in ((0, to_down), (1, to_up)):
            raw.append(
                remote(
                    ints.at[rows(far * pairs + side * half + c * CHUNK)],
                    via.at[side, rows(c * CHUNK), pl.ds(depth, depth)],
                    raw_send.at[side, c],
                    raw_recv.at[side, c],
                    device,
                )
            )
    halo = []
    for side, device in ((0, to_right), (1, to_left)):
        halo.append(
            remote(
                doms.at[rows(pairs, pairs)],
                doms.at[rows(side * 2 * pairs, pairs)],
                dom_send.at[side],
                dom_recv.at[side],
                device,
            )
        )
    for c in range(pairs // CHUNK):
        for side, device in ((0, to_right), (1, to_left)):
            halo.append(
                remote(
                    pao.at[rows(pairs + c * CHUNK)],
                    pao.at[rows(side * 2 * pairs + c * CHUNK)],
                    halo_send.at[side, c],
                    halo_recv.at[side, c],
                    device,
                )
            )
    for copy in raw + halo:
        copy.start()

    for copy in via_loads:
        copy.wait()
    sums = []
    for c in range(chunks):
        for side, device in ((0, to_down), (1, to_up)):
            raw[c * 2 + side].wait_recv()

            def add_up(i, carry, side=side, c=c):
                p = c * CHUNK + i
                block = via[side, p]
                summed[side, p] = contract(block[:, :width], block[:, width:], 0, 0).astype(BF16)
                return carry

            lax.fori_loop(0, CHUNK, add_up, 0)
            copy = remote(
                summed.at[side, rows(c * CHUNK)],
                arrived.at[rows(side * half + c * CHUNK)],
                summed_send.at[side, c],
                summed_recv.at[side, c],
                device,
            )
            copy.start()
            sums.append(copy)

    for copy in halo:
        copy.wait_send()

    near = []
    for c in range(chunks):
        for side, device, there in ((0, to_up, up), (1, to_down, down)):
            copy = remote(
                ints.at[rows(there * pairs + side * half + c * CHUNK)],
                own.at[rows(side * half + c * CHUNK), pl.ds(depth, depth)],
                near_send.at[side, c],
                near_recv.at[side, c],
                device,
            )
            copy.start()
            near.append(copy)

    for copy in halo:
        copy.wait_recv()

    first_row = ((pair * n_aux + aux) - 1) * pairs

    def couple(p, carry):
        mine = jnp.broadcast_to(doms[pl.ds(pairs + p, 1), :], (width, width)).T
        matches, scaled = [], []
        for k in range(slots):
            row = jnp.clip(neighbours[k, p] - first_row, 0, 3 * pairs - 1)
            weight = jnp.where(k < counts[p], couplings[k, p], 0.0)
            match = jnp.where(mine == doms[pl.ds(row, 1), :], 1.0, 0.0).astype(BF16)
            picked = contract(match, pao[row], 1, 0)
            matches.append(match)
            scaled.append((weight * picked).astype(BF16))
        total = contract(jnp.concatenate(scaled, axis=1), jnp.concatenate(matches, axis=1), 1, 1)
        c = coeffs[p]
        right_half = contract(total.astype(BF16), c, 1, 0).astype(BF16)
        acc[p] = contract(c, right_half, 0, 0)
        return carry

    lax.fori_loop(0, pairs, couple, 0)

    own_load.wait()
    stores = []
    for c in range(chunks):
        for side in (0, 1):
            near[c * 2 + side].wait_recv()
            sums[c * 2 + side].wait_recv()
            first = side * half + c * CHUNK

            def finish(i, carry, first=first):
                p = first + i
                block = own[p]
                acc[p] += contract(block[:, :width], block[:, width:], 0, 0) + arrived[p].astype(F32)
                return carry

            lax.fori_loop(0, CHUNK, finish, 0)
            copy = pltpu.make_async_copy(acc.at[rows(first)], out.at[rows(first)], out_sem.at[side, c])
            copy.start()
            stores.append(copy)

    for copy in raw + near + sums:
        copy.wait_send()
    for copy in stores:
        copy.wait()


def per_device(
    integrals,
    amplitudes,
    coeffs,
    domains,
    neighbours,
    counts,
    couplings,
    pno_energies,
    occ_energies,
):
    pairs, width, _ = amplitudes.shape
    depth = integrals.shape[1]
    half = pairs // 2
    chunks = half // CHUNK
    anywhere = pl.BlockSpec(memory_space=pl.ANY)
    scalars = pl.BlockSpec(memory_space=pltpu.SMEM)
    dma = pltpu.SemaphoreType.DMA
    gathered = pl.pallas_call(
        kernel,
        out_shape=jax.ShapeDtypeStruct((pairs, width, width), F32),
        in_specs=[anywhere] * 4 + [scalars] * 3,
        out_specs=anywhere,
        scratch_shapes=[
            pltpu.VMEM((pairs, width, width), BF16),
            pltpu.VMEM((pairs, width, width), BF16),
            pltpu.VMEM((3 * pairs, width, width), BF16),
            pltpu.VMEM((3 * pairs, width), jnp.int32),
            pltpu.VMEM((pairs, 2 * depth, 2 * width), BF16),
            pltpu.VMEM((2, half, 2 * depth, 2 * width), BF16),
            pltpu.VMEM((2, half, width, width), BF16),
            pltpu.VMEM((pairs, width, width), BF16),
            pltpu.VMEM((pairs, width, width), F32),
            dma((3,)),
            dma(()),
            dma((2,)),
            dma((2, chunks)),
            dma((2, chunks)),
            dma((2, chunks)),
            dma((2, chunks)),
            dma((2, chunks)),
            dma((2, chunks)),
            dma((2, 2 * chunks)),
            dma((2, 2 * chunks)),
            dma((2,)),
            dma((2,)),
            dma((2, chunks)),
        ],
        compiler_params=pltpu.CompilerParams(
            collective_id=0, has_side_effects=True, vmem_limit_bytes=32 * 1024 * 1024
        ),
        name="contract_and_couple",
    )(integrals, amplitudes, coeffs, domains, neighbours.T, counts, couplings.T)
    denominator = pno_energies[:, :, None] + pno_energies[:, None, :] + occ_energies[:, None, None]
    amps_wide = amplitudes.astype(F32)
    residual = gathered + denominator * amps_wide
    updated = (amps_wide - residual / denominator).astype(BF16)
    return (residual, updated)


def solution(mesh):
    in_specs = (
        P("pair", "aux", None),
        P(("pair", "aux"), None, None),
        P(("pair", "aux"), None, None),
        P(("pair", "aux"), None),
        P(("pair", "aux"), None),
        P(("pair", "aux")),
        P(("pair", "aux"), None),
        P(("pair", "aux"), None),
        P(("pair", "aux")),
    )
    out_specs = (P(("pair", "aux"), None, None), P(("pair", "aux"), None, None))
    return jax.shard_map(
        per_device, mesh=mesh, in_specs=in_specs, out_specs=out_specs, check_vma=False
    )
```

time: 101 us -> 57.4 us (0.57)
  the two profiles are of different devices: /device:TPU:485 before, /device:TPU:1 now
where the time goes in v1:
time: 57.4 us; the launch traced here: 57 us
  Pallas kernels  48.3 us (84%)
  local copies, waits for them, and re-layouts  6.4 us (11%)
  other arithmetic  1.64 us (3%)
  between operations  0.67 us (1%)
    pallas_call x1, Pallas kernels, per_device(): pl.pallas_call(kernel, out_shape=jax.ShapeDtypeStruct((pairs, width, widt...  48.3 us
    unnamed x18, local copies, waits for them, and re-layouts  6.4 us
    convert_element_type x1, other arithmetic, per_device(): updated = (amps_wide - residual / denominator).astype(BF16)  1.64 us

profile of v1, /device:TPU:1, one launch (start us, length us, event | category | flops | bytes accessed | tf_op | source)
XLA Modules:
  0.0 57.0 jit_solution(12931369423231931159)
XLA Ops:
  0.6 0.0 copy-start
  0.6 1.6 %copy-done = bf16[64,64,256]{2,1,0:T(8,128)(2,1)S(1)} copy-done((bf16[64,64,256]{2,1,0:T(8,128)(2,1)S(1)}, bf16[64,64,256]{2,1,0:T(8,128)(2,1)}, u32[]{:S(2)}) %copy-start) | copy-done | bytes 2097176
  2.2 0.0 copy-start.1
  2.2 1.0 %copy-done.1 = bf16[16,128,128]{2,1,0:T(8,128)(2,1)S(1)} copy-done((bf16[16,128,128]{2,1,0:T(8,128)(2,1)S(1)}, bf16[16,128,128]{2,1,0:T(8,128)(2,1)}, u32[]{:S(2)}) %copy-start.1) | copy-done | bytes 524312
  3.3 0.0 copy-start.2
  3.3 1.0 %copy-done.2 = bf16[16,128,128]{2,1,0:T(8,128)(2,1)S(1)} copy-done((bf16[16,128,128]{2,1,0:T(8,128)(2,1)S(1)}, bf16[16,128,128]{2,1,0:T(8,128)(2,1)}, u32[]{:S(2)}) %copy-start.2) | copy-done | bytes 524312
  4.3 0.0 copy-start.3
  4.3 0.7 %copy-done.3 = s32[16,128]{1,0:T(8,128)S(1)} copy-done((s32[16,128]{1,0:T(8,128)S(1)}, s32[16,128]{1,0:T(8,128)}, u32[]{:S(2)}) %copy-start.3) | copy-done | bytes 8216
  5.0 0.0 copy-start.4
  5.0 0.7 %copy-done.4 = s32[16,8]{0,1:T(8,128)S(1)} copy-done((s32[16,8]{0,1:T(8,128)S(1)}, s32[16,8]{0,1:T(8,128)}, u32[]{:S(2)}) %copy-start.4) | copy-done | bytes 536
  5.7 0.0 copy-start.5
  5.7 0.7 %copy-done.5 = f32[16,8]{0,1:T(8,128)S(1)} copy-done((f32[16,8]{0,1:T(8,128)S(1)}, f32[16,8]{0,1:T(8,128)}, u32[]{:S(2)}) %copy-start.5) | copy-done | bytes 536
  6.4 0.0 copy-start.6
  6.4 0.7 %copy-done.6 = s32[16]{0:T(128)S(1)} copy-done((s32[16]{0:T(128)S(1)}, s32[16]{0:T(128)}, u32[]{:S(2)}) %copy-start.6) | copy-done | bytes 88
  7.0 0.0 copy-start.7
  7.0 0.0 copy-start.8
  7.0 48.3 %contract_and_couple.1 = f32[16,128,128]{2,1,0:T(8,128)S(1)} custom-call(bf16[64,64,256]{2,1,0:T(8,128)(2,1)S(1)} %copy-done, bf16[16,128,128]{2,1,0:T(8,128)(2,1)S(1)} %copy-done.1, bf16[16,128,128]{2,1,0:T(8,128)(2,1)S(1)} %copy-done.2, s32[16,128]{1,0:T(8,128)S(1)} %copy-done.3, s32[8,16]{1,0:T(8,128)S(1)} %bitcast.2, s32[16]{0:T(128)S(1)} %copy-done.6, ...), custom_call_target="tpu_custom_call" | custom-call | tf_op jit(solution)/shard_map/contract_and_couple/pallas_call | solution.py:224
  55.3 0.0 copy-done.7
  55.4 0.0 copy-done.8
  55.4 1.6 %fusion.1 = (bf16[16,128,128]{2,1,0:T(8,128)(2,1)}, f32[16,128,128]{2,1,0:T(8,128)}) fusion(bf16[16,128,128]{2,1,0:T(8,128)(2,1)S(1)} %copy-done.1, f32[16]{0:T(128)S(1)} %copy-done.8, f32[16,128]{1,0:T(8,128)S(1)} %copy-done.7, f32[16,128,128]{2,1,0:T(8,128)S(1)} %contract_and_couple.1), kind=kLoop, calls=%fused_computation.3 | loop fusion | flops 2097152 | bytes 3153984 | tf_op jit(solution)/shard_map/convert_element_type | solution.py:262
Async XLA Ops:
  0.6 1.6 %copy-start = (bf16[64,64,256]{2,1,0:T(8,128)(2,1)S(1)}, bf16[64,64,256]{2,1,0:T(8,128)(2,1)}, u32[]{:S(2)}) copy-start(bf16[64,64,256]{2,1,0:T(8,128)(2,1)} %ints.1) | copy-start | bytes 6291460
  2.2 1.0 %copy-start.1 = (bf16[16,128,128]{2,1,0:T(8,128)(2,1)S(1)}, bf16[16,128,128]{2,1,0:T(8,128)(2,1)}, u32[]{:S(2)}) copy-start(bf16[16,128,128]{2,1,0:T(8,128)(2,1)} %amps_in.1) | copy-start | bytes 1572868
  3.3 1.0 %copy-start.2 = (bf16[16,128,128]{2,1,0:T(8,128)(2,1)S(1)}, bf16[16,128,128]{2,1,0:T(8,128)(2,1)}, u32[]{:S(2)}) copy-start(bf16[16,128,128]{2,1,0:T(8,128)(2,1)} %coeffs_in.1) | copy-start | bytes 1572868
  4.3 0.7 %copy-start.3 = (s32[16,128]{1,0:T(8,128)S(1)}, s32[16,128]{1,0:T(8,128)}, u32[]{:S(2)}) copy-start(s32[16,128]{1,0:T(8,128)} %domains_in.1) | copy-start | bytes 24580
  5.0 0.7 %copy-start.4 = (s32[16,8]{0,1:T(8,128)S(1)}, s32[16,8]{0,1:T(8,128)}, u32[]{:S(2)}) copy-start(s32[16,8]{0,1:T(8,128)} %param.13) | copy-start | bytes 1540
  5.7 0.7 %copy-start.5 = (f32[16,8]{0,1:T(8,128)S(1)}, f32[16,8]{0,1:T(8,128)}, u32[]{:S(2)}) copy-start(f32[16,8]{0,1:T(8,128)} %param.15) | copy-start | bytes 1540
  6.4 0.7 %copy-start.6 = (s32[16]{0:T(128)S(1)}, s32[16]{0:T(128)}, u32[]{:S(2)}) copy-start(s32[16]{0:T(128)} %counts.1) | copy-start | bytes 196
  7.0 48.3 %copy-start.7 = (f32[16,128]{1,0:T(8,128)S(1)}, f32[16,128]{1,0:T(8,128)}, u32[]{:S(2)}) copy-start(f32[16,128]{1,0:T(8,128)} %param.16) | copy-start | bytes 24580
  7.0 48.3 %copy-start.8 = (f32[16]{0:T(128)S(1)}, f32[16]{0:T(128)}, u32[]{:S(2)}) copy-start(f32[16]{0:T(128)} %param.17) | copy-start | bytes 196

commit v2 on v1

--- a/solution.py
+++ b/solution.py
@@ -16,9 +16,9 @@
 
 
 def kernel(
-    ints, amps_in, coeffs_in, domains_in, neighbours, counts, couplings,
+    ints, amps_in, coeffs_in, domains_in, neighbours_in, counts_in, couplings_in,
     out,
-    amps, coeffs, pao, doms, own, via, summed, arrived, acc,
+    amps, coeffs, pao, doms, neighbours, counts, couplings, own, via, summed, arrived, acc,
     load_sem, own_sem, via_sem, raw_send, raw_recv, near_send, near_recv,
     summed_send, summed_recv, halo_send, halo_recv, dom_send, dom_recv, out_sem,
 ):
@@ -53,6 +53,11 @@
         pltpu.make_async_copy(amps_in, amps, load_sem.at[1]),
         pltpu.make_async_copy(domains_in, doms.at[rows(pairs, pairs)], load_sem.at[2]),
     ]
+    scalar_loads = [
+        pltpu.make_async_copy(neighbours_in, neighbours, load_sem.at[3]),
+        pltpu.make_async_copy(counts_in, counts, load_sem.at[4]),
+        pltpu.make_async_copy(couplings_in, couplings, load_sem.at[5]),
+    ]
     via_loads = [
         pltpu.make_async_copy(
             ints.at[rows(down * pairs, half)], via.at[0, :, pl.ds(0, depth)], via_sem.at[0]
@@ -62,58 +67,58 @@
         ),
     ]
     own_load = pltpu.make_async_copy(ints.at[rows(aux * pairs, pairs)], own.at[:, pl.ds(0, depth)], own_sem)
-    for copy in loads + via_loads + [own_load]:
+    for copy in loads + via_loads + [own_load] + scalar_loads:
         copy.start()
 
+    pl.semaphore_wait(barrier, 4)
+
+    raw = []
+    for c in range(chunks):
+        for side, device in ((0, to_down), (1, to_up)):
+            copy = remote(
+                ints.at[rows(far * pairs + side * half + c * CHUNK)],
+                via.at[side, rows(c * CHUNK), pl.ds(depth, depth)],
+                raw_send.at[side, c],
+                raw_recv.at[side, c],
+                device,
+            )
+            copy.start()
+            raw.append(copy)
+
     for copy in loads:
         copy.wait()
 
-    def to_pao(p, carry):
-        c = coeffs[p]
-        left_half = contract(c, amps[p], 1, 0).astype(BF16)
-        pao[pairs + p] = contract(left_half, c, 1, 1).astype(BF16)
-        return carry
-
-    lax.fori_loop(0, pairs, to_pao, 0)
-
-    pl.semaphore_wait(barrier, 4)
-
-    raw = []
-    for c in range(chunks):
-        for side, device in ((0, to_down), (1, to_up)):
-            raw.append(
-                remote(
-                    ints.at[rows(far * pairs + side * half + c * CHUNK)],
-                    via.at[side, rows(c * CHUNK), pl.ds(depth, depth)],
-                    raw_send.at[side, c],
-                    raw_recv.at[side, c],
-                    device,
-                )
-            )
     halo = []
     for side, device in ((0, to_right), (1, to_left)):
-        halo.append(
-            remote(
-                doms.at[rows(pairs, pairs)],
-                doms.at[rows(side * 2 * pairs, pairs)],
-                dom_send.at[side],
-                dom_recv.at[side],
-                device,
-            )
+        copy = remote(
+            doms.at[rows(pairs, pairs)],
+            doms.at[rows(side * 2 * pairs, pairs)],
+            dom_send.at[side],
+            dom_recv.at[side],
+            device,
         )
+        copy.start()
+        halo.append(copy)
     for c in range(pairs // CHUNK):
+
+        def to_pao(i, carry, c=c):
+            p = c * CHUNK + i
+            block = coeffs[p]
+            left_half = contract(block, amps[p], 1, 0).astype(BF16)
+            pao[pairs + p] = contract(left_half, block, 1, 1).astype(BF16)
+            return carry
+
+        lax.fori_loop(0, CHUNK, to_pao, 0)
         for side, device in ((0, to_right), (1, to_left)):
-            halo.append(
-                remote(
-                    pao.at[rows(pairs + c * CHUNK)],
-                    pao.at[rows(side * 2 * pairs + c * CHUNK)],
-                    halo_send.at[side, c],
-                    halo_recv.at[side, c],
-                    device,
-                )
-            )
-    for copy in raw + halo:
-        copy.start()
+            copy = remote(
+                pao.at[rows(pairs + c * CHUNK)],
+                pao.at[rows(side * 2 * pairs + c * CHUNK)],
+                halo_send.at[side, c],
+                halo_recv.at[side, c],
+                device,
+            )
+            copy.start()
+            halo.append(copy)
 
     for copy in via_loads:
         copy.wait()
@@ -139,7 +144,7 @@
             copy.start()
             sums.append(copy)
 
-    for copy in halo:
+    for copy in halo[:-2]:
         copy.wait_send()
 
     near = []
@@ -155,8 +160,12 @@
             copy.start()
             near.append(copy)
 
+    halo[-2].wait_send()
+    halo[-1].wait_send()
     for copy in halo:
         copy.wait_recv()
+    for copy in scalar_loads:
+        copy.wait()
 
     first_row = ((pair * n_aux + aux) - 1) * pairs
 
@@ -219,24 +228,27 @@
     half = pairs // 2
     chunks = half // CHUNK
     anywhere = pl.BlockSpec(memory_space=pl.ANY)
-    scalars = pl.BlockSpec(memory_space=pltpu.SMEM)
+    in_hbm = pl.BlockSpec(memory_space=pltpu.HBM)
     dma = pltpu.SemaphoreType.DMA
     gathered = pl.pallas_call(
         kernel,
         out_shape=jax.ShapeDtypeStruct((pairs, width, width), F32),
-        in_specs=[anywhere] * 4 + [scalars] * 3,
+        in_specs=[in_hbm] * 7,
         out_specs=anywhere,
         scratch_shapes=[
             pltpu.VMEM((pairs, width, width), BF16),
             pltpu.VMEM((pairs, width, width), BF16),
             pltpu.VMEM((3 * pairs, width, width), BF16),
             pltpu.VMEM((3 * pairs, width), jnp.int32),
+            pltpu.SMEM(neighbours.shape[::-1], jnp.int32),
+            pltpu.SMEM(counts.shape, jnp.int32),
+            pltpu.SMEM(couplings.shape[::-1], F32),
             pltpu.VMEM((pairs, 2 * depth, 2 * width), BF16),
             pltpu.VMEM((2, half, 2 * depth, 2 * width), BF16),
             pltpu.VMEM((2, half, width, width), BF16),
             pltpu.VMEM((pairs, width, width), BF16),
             pltpu.VMEM((pairs, width, width), F32),
-            dma((3,)),
+            dma((6,)),
             dma(()),
             dma((2,)),
             dma((2, chunks)),
@@ -255,7 +267,12 @@
             collective_id=0, has_side_effects=True, vmem_limit_bytes=32 * 1024 * 1024
         ),
         name="contract_and_couple",
-    )(integrals, amplitudes, coeffs, domains, neighbours.T, counts, couplings.T)
+    )(
+        *(
+            pltpu.with_memory_space_constraint(operand, pltpu.HBM)
+            for operand in (integrals, amplitudes, coeffs, domains, neighbours.T, counts, couplings.T)
+        )
+    )
     denominator = pno_energies[:, :, None] + pno_energies[:, None, :] + occ_energies[:, None, None]
     amps_wide = amplitudes.astype(F32)
     residual = gathered + denominator * amps_wide

time: 57.4 us -> 48.5 us (0.84)
  local copies, waits for them, and re-layouts: 6.4 us -> 0.01 us
  Pallas kernels: 48.3 us -> 46.1 us
    unnamed x18 -> x6, local copies, waits for them, and re-layouts: 6.4 us -> 0.01 us
    pallas_call x1, Pallas kernels: 48.3 us -> 46.1 us  [per_device(): pl.pallas_call(kernel, out_shape=jax.ShapeDtypeStruct((pairs, width, widt...]
where the time goes in v2:
time: 48.5 us; the launch traced here: 48.4 us
  Pallas kernels  46.1 us (95%)
  other arithmetic  1.63 us (3%)
  between operations  0.69 us (1%)
    pallas_call x1, Pallas kernels, per_device(): pl.pallas_call(kernel, out_shape=jax.ShapeDtypeStruct((pairs, width, widt...  46.1 us
    convert_element_type x1, other arithmetic, per_device(): updated = (amps_wide - residual / denominator).astype(BF16)  1.63 us

profile of v2, /device:TPU:1, one launch (start us, length us, event | category | flops | bytes accessed | tf_op | source)
XLA Modules:
  0.0 48.4 jit_solution(15344919326158037994)
XLA Ops:
  0.6 0.0 copy-start
  0.6 0.0 copy-start.1
  0.7 0.0 copy-start.2
  0.7 46.1 %contract_and_couple.1 = f32[16,128,128]{2,1,0:T(8,128)S(1)} custom-call(bf16[64,64,256]{2,1,0:T(8,128)(2,1)} %ints.1, bf16[16,128,128]{2,1,0:T(8,128)(2,1)} %amps_in.1, bf16[16,128,128]{2,1,0:T(8,128)(2,1)} %coeffs_in.1, s32[16,128]{1,0:T(8,128)} %domains_in.1, s32[8,16]{1,0:T(8,128)} %bitcast.2, s32[16]{0:T(128)} %counts_in.1, f32[8,16]{1,0:T(8,128)} %bitcast.3), custom_call_target="tpu_custom_call" | custom-call | tf_op jit(solution)/shard_map/contract_and_couple/pallas_call | solution.py:233
  46.8 0.0 copy-done
  46.8 0.0 copy-done.1
  46.8 0.0 copy-done.2
  46.8 1.6 %fusion.1 = (bf16[16,128,128]{2,1,0:T(8,128)(2,1)}, f32[16,128,128]{2,1,0:T(8,128)}) fusion(bf16[16,128,128]{2,1,0:T(8,128)(2,1)S(1)} %copy-done, f32[16]{0:T(128)S(1)} %copy-done.2, f32[16,128]{1,0:T(8,128)S(1)} %copy-done.1, f32[16,128,128]{2,1,0:T(8,128)S(1)} %contract_and_couple.1), kind=kLoop, calls=%fused_computation.3 | loop fusion | flops 2097152 | bytes 3153984 | tf_op jit(solution)/shard_map/convert_element_type | solution.py:279
Async XLA Ops:
  0.6 46.1 %copy-start = (bf16[16,128,128]{2,1,0:T(8,128)(2,1)S(1)}, bf16[16,128,128]{2,1,0:T(8,128)(2,1)}, u32[]{:S(2)}) copy-start(bf16[16,128,128]{2,1,0:T(8,128)(2,1)} %amps_in.1) | copy-start | bytes 1572868
  0.6 46.1 %copy-start.1 = (f32[16,128]{1,0:T(8,128)S(1)}, f32[16,128]{1,0:T(8,128)}, u32[]{:S(2)}) copy-start(f32[16,128]{1,0:T(8,128)} %param.16) | copy-start | bytes 24580
  0.7 46.1 %copy-start.2 = (f32[16]{0:T(128)S(1)}, f32[16]{0:T(128)}, u32[]{:S(2)}) copy-start(f32[16]{0:T(128)} %param.17) | copy-start | bytes 196

commit v3 on v2

v3 whole, which is shorter than its diff:
```python
import jax
import jax.numpy as jnp
from jax import lax
from jax.experimental import pallas as pl
from jax.experimental.pallas import tpu as pltpu
from jax.sharding import PartitionSpec as P

MESH = pl.DeviceIdType.MESH
F32 = jnp.float32
BF16 = jnp.bfloat16
CHUNK = 4
TOGETHER = 4


def contract(a, b, dim_a, dim_b):
    return lax.dot_general(a, b, (((dim_a,), (dim_b,)), ((), ())), preferred_element_type=F32)


def kernel(
    ints, amps_in, coeffs_in, domains_in, neighbours_in, counts_in, couplings_in, pno_in, occ_in,
    residual, updated,
    amps, coeffs, pao, doms, neighbours, counts, couplings, pno, occ, own, via, summed, arrived, acc,
    load_sem, own_sem, via_sem, raw_send, raw_recv, near_send, near_recv,
    summed_send, summed_recv, halo_send, halo_recv, dom_send, dom_recv, pass_send, pass_dom_send,
):
    n_pair, n_aux = lax.axis_size("pair"), lax.axis_size("aux")
    pair, aux = lax.axis_index("pair"), lax.axis_index("aux")
    pairs = amps.shape[0]
    half = pairs // 2
    depth = ints.shape[1]
    width = amps.shape[1]
    slots = neighbours.shape[0]
    chunks = half // CHUNK
    all_chunks = pairs // CHUNK

    up, down, far = (aux + 1) % n_aux, (aux + n_aux - 1) % n_aux, (aux + 2) % n_aux
    to_up, to_down = (pair, up), (pair, down)
    next_pair, last_pair = ((pair + 1) % n_pair, aux), ((pair + n_pair - 1) % n_pair, aux)
    first_end, last_end = aux == 0, aux == n_aux - 1
    at_end = jnp.logical_or(first_end, last_end)

    barrier = pltpu.get_barrier_semaphore()

    def greet(device):
        pl.semaphore_signal(barrier, inc=1, device_id=device, device_id_type=MESH)

    greet(to_up)
    greet(to_down)

    @pl.when(at_end)
    def _():
        greet(next_pair)
        greet(last_pair)

    def remote(src, dst, send, recv, device):
        return pltpu.make_async_remote_copy(
            src_ref=src, dst_ref=dst, send_sem=send, recv_sem=recv, device_id=device, device_id_type=MESH
        )

    def rows(first, count=CHUNK):
        return pl.ds(first, count)

    loads = [
        pltpu.make_async_copy(coeffs_in, coeffs, load_sem.at[0]),
        pltpu.make_async_copy(amps_in, amps, load_sem.at[1]),
        pltpu.make_async_copy(domains_in, doms.at[rows(pairs, pairs)], load_sem.at[2]),
    ]
    small_loads = [
        pltpu.make_async_copy(neighbours_in, neighbours, load_sem.at[3]),
        pltpu.make_async_copy(counts_in, counts, load_sem.at[4]),
        pltpu.make_async_copy(couplings_in, couplings, load_sem.at[5]),
        pltpu.make_async_copy(pno_in, pno, load_sem.at[6]),
        pltpu.make_async_copy(occ_in, occ, load_sem.at[7]),
    ]
    via_loads = [
        pltpu.make_async_copy(
            ints.at[rows(down * pairs, half)], via.at[0, :, pl.ds(0, depth)], via_sem.at[0]
        ),
        pltpu.make_async_copy(
            ints.at[rows(up * pairs + half, half)], via.at[1, :, pl.ds(0, depth)], via_sem.at[1]
        ),
    ]
    own_load = pltpu.make_async_copy(ints.at[rows(aux * pairs, pairs)], own.at[:, pl.ds(0, depth)], own_sem)
    for copy in loads + via_loads + [own_load] + small_loads:
        copy.start()

    pl.semaphore_wait(barrier, jnp.where(at_end, 4, 2))

    raw = []
    for c in range(chunks):
        for side, device in ((0, to_down), (1, to_up)):
            copy = remote(
                ints.at[rows(far * pairs + side * half + c * CHUNK)],
                via.at[side, rows(c * CHUNK), pl.ds(depth, depth)],
                raw_send.at[side, c],
                raw_recv.at[side, c],
                device,
            )
            copy.start()
            raw.append(copy)

    for copy in loads:
        copy.wait()

    targets = (
        (0, to_up, jnp.where(last_end, 3, 0)),
        (1, to_down, jnp.where(first_end, 3, 2)),
    )
    halo = []
    for side, device, part in targets:
        copy = remote(
            doms.at[rows(pairs, pairs)],
            doms.at[rows(part * pairs, pairs)],
            dom_send.at[side],
            dom_recv.at[part],
            device,
        )
        copy.start()
        halo.append(copy)
    for c in range(all_chunks):
        here = [c * CHUNK + i for i in range(CHUNK)]
        left_half = [contract(coeffs[p], amps[p], 1, 0).astype(BF16) for p in here]
        for p, block in zip(here, left_half):
            pao[pairs + p] = contract(block, coeffs[p], 1, 1).astype(BF16)
        for side, device, part in targets:
            copy = remote(
                pao.at[rows(pairs + c * CHUNK)],
                pao.at[rows(part * pairs + c * CHUNK)],
                halo_send.at[side, c],
                halo_recv.at[part, c],
                device,
            )
            copy.start()
            halo.append(copy)

    for copy in via_loads:
        copy.wait()
    sums = []
    for c in range(chunks):
        for side, device in ((0, to_down), (1, to_up)):
            raw[c * 2 + side].wait_recv()
            for p in range(c * CHUNK, c * CHUNK + CHUNK):
                block = via[side, p]
                summed[side, p] = contract(block[:, :width], block[:, width:], 0, 0).astype(BF16)
            copy = remote(
                summed.at[side, rows(c * CHUNK)],
                arrived.at[rows(side * half + c * CHUNK)],
                summed_send.at[side, c],
                summed_recv.at[side, c],
                device,
            )
            copy.start()
            sums.append(copy)

    def pass_on(device, part):
        passed = [
            remote(
                doms.at[rows(3 * pairs, pairs)],
                doms.at[rows(part * pairs, pairs)],
                pass_dom_send,
                dom_recv.at[part],
                device,
            )
        ]
        passed[0].start()
        for c in range(all_chunks):
            arrival(3, c).wait_recv()
            copy = remote(
                pao.at[rows(3 * pairs + c * CHUNK)],
                pao.at[rows(part * pairs + c * CHUNK)],
                pass_send.at[c],
                halo_recv.at[part, c],
                device,
            )
            copy.start()
            passed.append(copy)
        return passed

    def arrival(part, c):
        return remote(
            pao.at[rows(pairs + c * CHUNK)],
            pao.at[rows(part * pairs + c * CHUNK)],
            halo_send.at[0, c],
            halo_recv.at[part, c],
            to_up,
        )

    def domain_arrival(part):
        return remote(
            doms.at[rows(pairs, pairs)], doms.at[rows(part * pairs, pairs)], dom_send.at[0], dom_recv.at[part], to_up
        )

    @pl.when(first_end)
    def _():
        domain_arrival(3).wait_recv()
        pass_on(next_pair, 0)

    @pl.when(last_end)
    def _():
        domain_arrival(3).wait_recv()
        pass_on(last_pair, 2)

    for copy in halo[:-2]:
        copy.wait_send()

    near = []
    for c in range(chunks):
        for side, device, there in ((0, to_up, up), (1, to_down, down)):
            copy = remote(
                ints.at[rows(there * pairs + side * half + c * CHUNK)],
                own.at[rows(side * half + c * CHUNK), pl.ds(depth, depth)],
                near_send.at[side, c],
                near_recv.at[side, c],
                device,
            )
            copy.start()
            near.append(copy)

    halo[-2].wait_send()
    halo[-1].wait_send()
    for copy in small_loads:
        copy.wait()
    for part in (0, 2):
        domain_arrival(part).wait_recv()
        for c in range(all_chunks):
            arrival(part, c).wait_recv()

    first_row = ((pair * n_aux + aux) - 1) * pairs

    def couple(step, carry):
        here = [step * TOGETHER + i for i in range(TOGETHER)]
        totals = []
        for p in here:
            mine = jnp.broadcast_to(doms[pl.ds(pairs + p, 1), :], (width, width)).T
            matches, scaled = [], []
            for k in range(slots):
                row = jnp.clip(neighbours[k, p] - first_row, 0, 3 * pairs - 1)
                weight = jnp.where(k < counts[p], couplings[k, p], 0.0)
                match = jnp.where(mine == doms[pl.ds(row, 1), :], 1.0, 0.0).astype(BF16)
                picked = contract(match, pao[row], 1, 0)
                matches.append(match)
                scaled.append((weight * picked).astype(BF16))
            total = contract(jnp.concatenate(scaled, axis=1), jnp.concatenate(matches, axis=1), 1, 1)
            totals.append(total.astype(BF16))
        halves = [contract(total, coeffs[p], 1, 0).astype(BF16) for p, total in zip(here, totals)]
        for p, right_half in zip(here, halves):
            acc[p] = contract(coeffs[p], right_half, 0, 0)
        return carry

    lax.fori_loop(0, pairs // TOGETHER, couple, 0)

    own_load.wait()
    for c in range(chunks):
        for side in (0, 1):
            near[c * 2 + side].wait_recv()
            sums[c * 2 + side].wait_recv()
            first = side * half + c * CHUNK
            for p in range(first, first + CHUNK):
                block = own[p]
                exchange = contract(block[:, :width], block[:, width:], 0, 0) + arrived[p].astype(F32)
                energies = jnp.broadcast_to(pno[pl.ds(p, 1), :], (width, width))
                denominator = energies.T + energies + occ[p]
                wide = amps[p].astype(F32)
                result = exchange + denominator * wide + acc[p]
                residual[p] = result
                updated[p] = (wide - result / denominator).astype(BF16)

    for copy in raw + near + sums:
        copy.wait_send()

    @pl.when(at_end)
    def _():
        domain_pass = remote(
            doms.at[rows(3 * pairs, pairs)], doms.at[rows(0, pairs)], pass_dom_send, dom_recv.at[0], next_pair
        )
        domain_pass.wait_send()
        for c in range(all_chunks):
            remote(
                pao.at[rows(3 * pairs + c * CHUNK)],
                pao.at[rows(c * CHUNK)],
                pass_send.at[c],
                halo_recv.at[0, c],
                next_pair,
            ).wait_send()


def per_device(
    integrals,
    amplitudes,
    coeffs,
    domains,
    neighbours,
    counts,
    couplings,
    pno_energies,
    occ_energies,
):
    pairs, width, _ = amplitudes.shape
    depth = integrals.shape[1]
    half = pairs // 2
    chunks = half // CHUNK
    in_hbm = pl.BlockSpec(memory_space=pltpu.HBM)
    in_vmem = pl.BlockSpec(memory_space=pltpu.VMEM)
    dma = pltpu.SemaphoreType.DMA
    operands = (
        integrals, amplitudes, coeffs, domains, neighbours.T, counts, couplings.T, pno_energies, occ_energies,
    )
    residual, updated = pl.pallas_call(
        kernel,
        out_shape=(
            pltpu.VMEM((pairs, width, width), F32),
            pltpu.VMEM((pairs, width, width), BF16),
        ),
        in_specs=[in_hbm] * len(operands),
        out_specs=(in_vmem, in_vmem),
        scratch_shapes=[
            pltpu.VMEM((pairs, width, width), BF16),
            pltpu.VMEM((pairs, width, width), BF16),
            pltpu.VMEM((4 * pairs, width, width), BF16),
            pltpu.VMEM((4 * pairs, width), jnp.int32),
            pltpu.SMEM(neighbours.shape[::-1], jnp.int32),
            pltpu.SMEM(counts.shape, jnp.int32),
            pltpu.SMEM(couplings.shape[::-1], F32),
            pltpu.VMEM(pno_energies.shape, F32),
            pltpu.SMEM(occ_energies.shape, F32),
            pltpu.VMEM((pairs, 2 * depth, 2 * width), BF16),
            pltpu.VMEM((2, half, 2 * depth, 2 * width), BF16),
            pltpu.VMEM((2, half, width, width), BF16),
            pltpu.VMEM((pairs, width, width), BF16),
            pltpu.VMEM((pairs, width, width), F32),
            dma((8,)),
            dma(()),
            dma((2,)),
            dma((2, chunks)),
            dma((2, chunks)),
            dma((2, chunks)),
            dma((2, chunks)),
            dma((2, chunks)),
            dma((2, chunks)),
            dma((2, 2 * chunks)),
            dma((4, 2 * chunks)),
            dma((2,)),
            dma((4,)),
            dma((2 * chunks,)),
            dma(()),
        ],
        compiler_params=pltpu.CompilerParams(
            collective_id=0, has_side_effects=True, vmem_limit_bytes=32 * 1024 * 1024
        ),
        name="doubles_residual",
    )(*(pltpu.with_memory_space_constraint(operand, pltpu.HBM) for operand in operands))
    return (residual, updated)


def solution(mesh):
    in_specs = (
        P("pair", "aux", None),
        P(("pair", "aux"), None, None),
        P(("pair", "aux"), None, None),
        P(("pair", "aux"), None),
        P(("pair", "aux"), None),
        P(("pair", "aux")),
        P(("pair", "aux"), None),
        P(("pair", "aux"), None),
        P(("pair", "aux")),
    )
    out_specs = (P(("pair", "aux"), None, None), P(("pair", "aux"), None, None))
    return jax.shard_map(
        per_device, mesh=mesh, in_specs=in_specs, out_specs=out_specs, check_vma=False
    )
```

time: 48.5 us -> 42.3 us (0.87)
  the two profiles are of different devices: /device:TPU:1 before, /device:TPU:6 now
where the time goes in v3:
time: 42.3 us; the launch traced here: 42.2 us
  Pallas kernels  39.8 us (94%)
  local copies, waits for them, and re-layouts  1.77 us (4%)
  between operations  0.64 us (2%)
    pallas_call x1, Pallas kernels, per_device(): pl.pallas_call(kernel, out_shape=(pltpu.VMEM((pairs, width, width), F32),...  39.8 us
    unnamed x2, local copies, waits for them, and re-layouts  1.77 us

profile of v3, /device:TPU:6, one launch (start us, length us, event | category | flops | bytes accessed | tf_op | source)
XLA Modules:
  0.0 42.2 jit_solution(2534145777677716211)
XLA Ops:
  0.6 39.8 %doubles_residual.1 = (f32[16,128,128]{2,1,0:T(8,128)S(1)}, bf16[16,128,128]{2,1,0:T(8,128)(2,1)S(1)}) custom-call(bf16[64,64,256]{2,1,0:T(8,128)(2,1)} %ints.1, bf16[16,128,128]{2,1,0:T(8,128)(2,1)} %amps_in.1, bf16[16,128,128]{2,1,0:T(8,128)(2,1)} %coeffs_in.1, s32[16,128]{1,0:T(8,128)} %domains_in.1, s32[8,16]{1,0:T(8,128)} %bitcast.2, s32[16]{0:T(128)} %counts_in.1, ...), custom_call_target="tpu_custom_call" | custom-call | tf_op jit(solution)/shard_map/doubles_residual/pallas_call | solution.py:308
  40.4 1.0 %copy.13 = f32[16,128,128]{2,1,0:T(8,128)} copy(f32[16,128,128]{2,1,0:T(8,128)S(1)} %get-tuple-element.2) | data formatting | bytes 2097152
  41.4 0.8 %copy.14 = bf16[16,128,128]{2,1,0:T(8,128)(2,1)} copy(bf16[16,128,128]{2,1,0:T(8,128)(2,1)S(1)} %get-tuple-element.3) | data formatting | bytes 1048576

commit v4 on v3

v4 whole, which is shorter than its diff:
```python
import jax
import jax.numpy as jnp
from jax import lax
from jax.experimental import pallas as pl
from jax.experimental.pallas import tpu as pltpu
from jax.sharding import PartitionSpec as P

MESH = pl.DeviceIdType.MESH
F32 = jnp.float32
BF16 = jnp.bfloat16
CHUNK = 4
TOGETHER = 4


def contract(a, b, dim_a, dim_b):
    return lax.dot_general(a, b, (((dim_a,), (dim_b,)), ((), ())), preferred_element_type=F32)


def kernel(
    ints, amps_in, coeffs_in, domains_in, neighbours_in, counts_in, couplings_in, pno_in, occ_in,
    residual, updated,
    amps, coeffs, pao, doms, neighbours, counts, couplings, pno, occ, own, via, summed, arrived,
    acc, inverse, mine, flipped,
    amps_sem, coeffs_sem, load_sem, own_sem, via_sem, raw_send, raw_recv, near_send, near_recv,
    summed_send, summed_recv, halo_send, halo_recv, dom_send, dom_recv, pass_send, pass_dom_send, ready,
):
    n_pair, n_aux = lax.axis_size("pair"), lax.axis_size("aux")
    pair, aux = lax.axis_index("pair"), lax.axis_index("aux")
    pairs = amps.shape[0]
    half = pairs // 2
    depth = ints.shape[1]
    width = amps.shape[1]
    slots = neighbours.shape[0]
    chunks = half // CHUNK
    all_chunks = pairs // CHUNK

    up, down, far = (aux + 1) % n_aux, (aux + n_aux - 1) % n_aux, (aux + 2) % n_aux
    to_up, to_down = (pair, up), (pair, down)
    next_pair, last_pair = ((pair + 1) % n_pair, aux), ((pair + n_pair - 1) % n_pair, aux)
    first_end, last_end = aux == 0, aux == n_aux - 1
    at_end = jnp.logical_or(first_end, last_end)
    no_left = jnp.logical_and(first_end, pair == 0)
    no_right = jnp.logical_and(last_end, pair == n_pair - 1)
    passes = jnp.logical_or(
        jnp.logical_and(first_end, pair < n_pair - 1), jnp.logical_and(last_end, pair > 0)
    )

    barrier = pltpu.get_barrier_semaphore()

    def greet(semaphore, device):
        pl.semaphore_signal(semaphore, inc=1, device_id=device, device_id_type=MESH)

    greet(barrier, to_up)
    greet(barrier, to_down)

    @pl.when(at_end)
    def _():
        greet(barrier, last_pair)

    def remote(src, dst, send, recv, device):
        return pltpu.make_async_remote_copy(
            src_ref=src, dst_ref=dst, send_sem=send, recv_sem=recv, device_id=device, device_id_type=MESH
        )

    def rows(first, count=CHUNK):
        return pl.ds(first, count)

    matrix_loads = []
    for c in range(all_chunks):
        part = rows(c * CHUNK)
        matrix_loads.append(
            [
                pltpu.make_async_copy(coeffs_in.at[part], coeffs.at[part], coeffs_sem.at[c]),
                pltpu.make_async_copy(amps_in.at[part], amps.at[part], amps_sem.at[c]),
            ]
        )
    domain_load = pltpu.make_async_copy(domains_in, doms.at[rows(pairs, pairs)], load_sem.at[0])
    small_loads = [
        pltpu.make_async_copy(neighbours_in, neighbours, load_sem.at[1]),
        pltpu.make_async_copy(counts_in, counts, load_sem.at[2]),
        pltpu.make_async_copy(couplings_in, couplings, load_sem.at[3]),
        pltpu.make_async_copy(pno_in, pno, load_sem.at[4]),
        pltpu.make_async_copy(occ_in, occ, load_sem.at[5]),
    ]
    via_loads = [
        pltpu.make_async_copy(
            ints.at[rows(down * pairs, half)], via.at[0, :, pl.ds(0, depth)], via_sem.at[0]
        ),
        pltpu.make_async_copy(
            ints.at[rows(up * pairs + half, half)], via.at[1, :, pl.ds(0, depth)], via_sem.at[1]
        ),
    ]
    own_load = pltpu.make_async_copy(ints.at[rows(aux * pairs, pairs)], own.at[:, pl.ds(0, depth)], own_sem)
    for copy in sum(matrix_loads, []) + [domain_load] + small_loads + [own_load] + via_loads:
        copy.start()

    def to_pao(c):
        for copy in matrix_loads[c]:
            copy.wait()
        here = [c * CHUNK + i for i in range(CHUNK)]
        left_half = [contract(coeffs[p], amps[p], 1, 0).astype(BF16) for p in here]
        for p, block in zip(here, left_half):
            pao[pairs + p] = contract(block, coeffs[p], 1, 1).astype(BF16)

    early = all_chunks // 2
    for c in range(early):
        to_pao(c)
    domain_load.wait()

    pl.semaphore_wait(barrier, jnp.where(at_end, 3, 2))

    @pl.when(jnp.logical_and(last_end, pair < n_pair - 1))
    def _():
        greet(ready, next_pair)

    targets = (
        (0, to_up, jnp.where(last_end, 3, 0)),
        (1, to_down, jnp.where(first_end, 3, 2)),
    )
    domain_halo = [
        remote(
            doms.at[rows(pairs, pairs)],
            doms.at[rows(part * pairs, pairs)],
            dom_send.at[side],
            dom_recv.at[part],
            device,
        )
        for side, device, part in targets
    ]
    for copy in domain_halo:
        copy.start()
    halo = []
    for c in range(all_chunks):
        if c >= early:
            to_pao(c)
        halo.append(
            [
                remote(
                    pao.at[rows(pairs + c * CHUNK)],
                    pao.at[rows(part * pairs + c * CHUNK)],
                    halo_send.at[side, c],
                    halo_recv.at[part, c],
                    device,
                )
                for side, device, part in targets
            ]
        )
        for copy in halo[c]:
            copy.start()

    def arrival(part, c):
        return remote(
            pao.at[rows(pairs + c * CHUNK)],
            pao.at[rows(part * pairs + c * CHUNK)],
            halo_send.at[0, c],
            halo_recv.at[part, c],
            to_up,
        )

    def domain_arrival(part):
        return remote(
            doms.at[rows(pairs, pairs)], doms.at[rows(part * pairs, pairs)], dom_send.at[0], dom_recv.at[part], to_up
        )

    pass_to = (jnp.where(first_end, next_pair[0], last_pair[0]), aux)
    pass_part = jnp.where(first_end, 0, 2)
    domain_pass = remote(
        doms.at[rows(3 * pairs, pairs)],
        doms.at[rows(pass_part * pairs, pairs)],
        pass_dom_send,
        dom_recv.at[pass_part],
        pass_to,
    )
    passed = [
        remote(
            pao.at[rows(3 * pairs + c * CHUNK)],
            pao.at[rows(pass_part * pairs + c * CHUNK)],
            pass_send.at[c],
            halo_recv.at[pass_part, c],
            pass_to,
        )
        for c in range(all_chunks)
    ]

    def halo_sent(c):
        for copy in halo[c]:
            copy.wait_send()

        @pl.when(at_end)
        def _():
            if c == 0:
                domain_arrival(3).wait_recv()
            arrival(3, c).wait_recv()

        if c == 0:

            @pl.when(jnp.logical_and(last_end, pair > 0))
            def _():
                pl.semaphore_wait(ready, 1)

        @pl.when(passes)
        def _():
            if c == 0:
                domain_pass.start()
            passed[c].start()

    def prepare(first, count):
        for p in range(first, first + count):
            energies = jnp.broadcast_to(pno[pl.ds(p, 1), :], (width, width))
            denominator = energies.T + energies + occ[p]
            inverse[p] = 1.0 / denominator
            block = own[p, pl.ds(0, depth), :]
            exchange = contract(block[:, :width], block[:, width:], 0, 0)
            acc[p] = exchange + denominator * amps[p].astype(F32)
            mine[p] = jnp.broadcast_to(doms[pl.ds(pairs + p, 1), :], (width, width)).T
            flipped[p] = coeffs[p].T

    for copy in small_loads:
        copy.wait()
    own_load.wait()
    prepare(0, half)
    for c in range(early):
        halo_sent(c)

    raw = []
    for c in range(chunks):
        for side, device in ((0, to_down), (1, to_up)):
            copy = remote(
                ints.at[rows(far * pairs + side * half + c * CHUNK)],
                via.at[side, rows(c * CHUNK), pl.ds(depth, depth)],
                raw_send.at[side, c],
                raw_recv.at[side, c],
                device,
            )
            copy.start()
            raw.append(copy)

    prepare(half, pairs - half)
    for c in range(early, all_chunks):
        halo_sent(c)

    for copy in via_loads:
        copy.wait()
    near, sums = [], []
    for c in range(chunks):
        for side, device, there in ((0, to_up, up), (1, to_down, down)):
            copy = remote(
                ints.at[rows(there * pairs + side * half + c * CHUNK)],
                own.at[rows(side * half + c * CHUNK), pl.ds(depth, depth)],
                near_send.at[side, c],
                near_recv.at[side, c],
                device,
            )
            copy.start()
            near.append(copy)
        for side, device in ((0, to_down), (1, to_up)):
            raw[c * 2 + side].wait_recv()
            for p in range(c * CHUNK, c * CHUNK + CHUNK):
                block = via[side, p]
                summed[side, p] = contract(block[:, :width], block[:, width:], 0, 0).astype(BF16)
            copy = remote(
                summed.at[side, rows(c * CHUNK)],
                arrived.at[rows(side * half + c * CHUNK)],
                summed_send.at[side, c],
                summed_recv.at[side, c],
                device,
            )
            copy.start()
            sums.append(copy)

    for part, none in ((0, no_left), (2, no_right)):

        @pl.when(jnp.logical_not(none))
        def _():
            domain_arrival(part).wait_recv()
            for c in range(all_chunks):
                arrival(part, c).wait_recv()

        @pl.when(none)
        def _():
            doms[pl.ds(part * pairs, pairs), :] = jnp.full((pairs, width), -1, jnp.int32)
            pao[pl.ds(part * pairs, pairs)] = jnp.zeros((pairs, width, width), BF16)

    first_row = ((pair * n_aux + aux) - 1) * pairs

    def couple(step, carry):
        here = [step * TOGETHER + i for i in range(TOGETHER)]
        totals = []
        for p in here:
            column = mine[p]
            matches, scaled = [], []
            for k in range(slots):
                row = jnp.clip(neighbours[k, p] - first_row, 0, 3 * pairs - 1)
                weight = jnp.where(k < counts[p], couplings[k, p], 0.0)
                match = jnp.where(column == doms[pl.ds(row, 1), :], 1.0, 0.0).astype(BF16)
                picked = contract(match, pao[row], 1, 0)
                matches.append(match)
                scaled.append((weight * picked).astype(BF16))
            total = contract(jnp.concatenate(scaled, axis=1), jnp.concatenate(matches, axis=1), 1, 1)
            totals.append(total.astype(BF16))
        halves = [contract(total, coeffs[p], 1, 0).astype(BF16) for p, total in zip(here, totals)]
        for p, right_half in zip(here, halves):
            acc[p] += contract(flipped[p], right_half, 1, 0)
        return carry

    lax.fori_loop(0, pairs // TOGETHER, couple, 0)

    for c in range(chunks):
        for side in (0, 1):
            near[c * 2 + side].wait_recv()
            sums[c * 2 + side].wait_recv()
            first = side * half + c * CHUNK
            for p in range(first, first + CHUNK):
                block = own[p, pl.ds(depth, depth), :]
                exchange = contract(block[:, :width], block[:, width:], 0, 0) + arrived[p].astype(F32)
                result = acc[p] + exchange
                residual[p] = result
                updated[p] = (amps[p].astype(F32) - result * inverse[p]).astype(BF16)

    for copy in raw + near + sums + domain_halo:
        copy.wait_send()

    @pl.when(passes)
    def _():
        for copy in [domain_pass] + passed:
            copy.wait_send()


def per_device(
    integrals,
    amplitudes,
    coeffs,
    domains,
    neighbours,
    counts,
    couplings,
    pno_energies,
    occ_energies,
):
    pairs, width, _ = amplitudes.shape
    depth = integrals.shape[1]
    half = pairs // 2
    chunks = half // CHUNK
    in_hbm = pl.BlockSpec(memory_space=pltpu.HBM)
    in_vmem = pl.BlockSpec(memory_space=pltpu.VMEM)
    dma = pltpu.SemaphoreType.DMA
    operands = (
        integrals, amplitudes, coeffs, domains, neighbours.T, counts, couplings.T, pno_energies, occ_energies,
    )
    residual, updated = pl.pallas_call(
        kernel,
        out_shape=(
            pltpu.VMEM((pairs, width, width), F32),
            pltpu.VMEM((pairs, width, width), BF16),
        ),
        in_specs=[in_hbm] * len(operands),
        out_specs=(in_vmem, in_vmem),
        scratch_shapes=[
            pltpu.VMEM((pairs, width, width), BF16),
            pltpu.VMEM((pairs, width, width), BF16),
            pltpu.VMEM((4 * pairs, width, width), BF16),
            pltpu.VMEM((4 * pairs, width), jnp.int32),
            pltpu.SMEM(neighbours.shape[::-1], jnp.int32),
            pltpu.SMEM(counts.shape, jnp.int32),
            pltpu.SMEM(couplings.shape[::-1], F32),
            pltpu.VMEM(pno_energies.shape, F32),
            pltpu.SMEM(occ_energies.shape, F32),
            pltpu.VMEM((pairs, 2 * depth, 2 * width), BF16),
            pltpu.VMEM((2, half, 2 * depth, 2 * width), BF16),
            pltpu.VMEM((2, half, width, width), BF16),
            pltpu.VMEM((pairs, width, width), BF16),
            pltpu.VMEM((pairs, width, width), F32),
            pltpu.VMEM((pairs, width, width), F32),
            pltpu.VMEM((pairs, width, width), jnp.int32),
            pltpu.VMEM((pairs, width, width), BF16),
            dma((2 * chunks,)),
            dma((2 * chunks,)),
            dma((6,)),
            dma(()),
            dma((2,)),
            dma((2, chunks)),
            dma((2, chunks)),
            dma((2, chunks)),
            dma((2, chunks)),
            dma((2, chunks)),
            dma((2, chunks)),
            dma((2, 2 * chunks)),
            dma((4, 2 * chunks)),
            dma((2,)),
            dma((4,)),
            dma((2 * chunks,)),
            dma(()),
            pltpu.SemaphoreType.REGULAR,
        ],
        compiler_params=pltpu.CompilerParams(
            collective_id=0, has_side_effects=True, vmem_limit_bytes=32 * 1024 * 1024
        ),
        name="doubles_residual",
    )(*(pltpu.with_memory_space_constraint(operand, pltpu.HBM) for operand in operands))
    return (residual, updated)


def solution(mesh):
    in_specs = (
        P("pair", "aux", None),
        P(("pair", "aux"), None, None),
        P(("pair", "aux"), None, None),
        P(("pair", "aux"), None),
        P(("pair", "aux"), None),
        P(("pair", "aux")),
        P(("pair", "aux"), None),
        P(("pair", "aux"), None),
        P(("pair", "aux")),
    )
    out_specs = (P(("pair", "aux"), None, None), P(("pair", "aux"), None, None))
    return jax.shard_map(
        per_device, mesh=mesh, in_specs=in_specs, out_specs=out_specs, check_vma=False
    )
```

time: 42.3 us -> 38.7 us (0.915)
  Pallas kernels: 39.8 us -> 35.8 us
    pallas_call x1, Pallas kernels: 39.8 us -> 35.8 us  [per_device(): pl.pallas_call(kernel, out_shape=(pltpu.VMEM((pairs, width, width), F32),...]
where the time goes in v4:
time: 38.7 us; the launch traced here: 38.2 us
  Pallas kernels  35.8 us (93%)
  local copies, waits for them, and re-layouts  1.77 us (5%)
  between operations  0.64 us (2%)
    pallas_call x1, Pallas kernels, per_device(): pl.pallas_call(kernel, out_shape=(pltpu.VMEM((pairs, width, width), F32),...  35.8 us
    unnamed x2, local copies, waits for them, and re-layouts  1.77 us

profile of v4, /device:TPU:6, one launch (start us, length us, event | category | flops | bytes accessed | tf_op | source)
XLA Modules:
  0.0 38.2 jit_solution(277728103422697962)
XLA Ops:
  0.6 35.8 %doubles_residual.1 = (f32[16,128,128]{2,1,0:T(8,128)S(1)}, bf16[16,128,128]{2,1,0:T(8,128)(2,1)S(1)}) custom-call(bf16[64,64,256]{2,1,0:T(8,128)(2,1)} %ints.1, bf16[16,128,128]{2,1,0:T(8,128)(2,1)} %amps_in.1, bf16[16,128,128]{2,1,0:T(8,128)(2,1)} %coeffs_in.1, s32[16,128]{1,0:T(8,128)} %domains_in.1, s32[8,16]{1,0:T(8,128)} %bitcast.2, s32[16]{0:T(128)} %counts_in.1, ...), custom_call_target="tpu_custom_call" | custom-call | tf_op jit(solution)/shard_map/doubles_residual/pallas_call | solution.py:350
  36.5 1.0 %copy.13 = f32[16,128,128]{2,1,0:T(8,128)} copy(f32[16,128,128]{2,1,0:T(8,128)S(1)} %get-tuple-element.2) | data formatting | bytes 2097152
  37.5 0.8 %copy.14 = bf16[16,128,128]{2,1,0:T(8,128)(2,1)} copy(bf16[16,128,128]{2,1,0:T(8,128)(2,1)S(1)} %get-tuple-element.3) | data formatting | bytes 1048576

commit v5 on v4

--- a/solution.py
+++ b/solution.py
@@ -129,24 +129,28 @@
     ]
     for copy in domain_halo:
         copy.start()
-    halo = []
-    for c in range(all_chunks):
-        if c >= early:
-            to_pao(c)
-        halo.append(
-            [
-                remote(
-                    pao.at[rows(pairs + c * CHUNK)],
-                    pao.at[rows(part * pairs + c * CHUNK)],
-                    halo_send.at[side, c],
-                    halo_recv.at[part, c],
-                    device,
-                )
-                for side, device, part in targets
-            ]
-        )
+    halo = [
+        [
+            remote(
+                pao.at[rows(pairs + c * CHUNK)],
+                pao.at[rows(part * pairs + c * CHUNK)],
+                halo_send.at[side, c],
+                halo_recv.at[part, c],
+                device,
+            )
+            for side, device, part in targets
+        ]
+        for c in range(all_chunks)
+    ]
+
+    def send_halo(c):
         for copy in halo[c]:
             copy.start()
+
+    for c in range(early):
+        send_halo(c)
+    for c in range(early, all_chunks):
+        to_pao(c)
 
     def arrival(part, c):
         return remote(
@@ -215,58 +219,51 @@
             mine[p] = jnp.broadcast_to(doms[pl.ds(pairs + p, 1), :], (width, width)).T
             flipped[p] = coeffs[p].T
 
+    raw = [
+        remote(
+            ints.at[rows(far * pairs + side * half + c * CHUNK)],
+            via.at[side, rows(c * CHUNK), pl.ds(depth, depth)],
+            raw_send.at[side, c],
+            raw_recv.at[side, c],
+            device,
+        )
+        for c in range(chunks)
+        for side, device in ((0, to_down), (1, to_up))
+    ]
+    near = [
+        remote(
+            ints.at[rows(there * pairs + side * half + c * CHUNK)],
+            own.at[rows(side * half + c * CHUNK), pl.ds(depth, depth)],
+            near_send.at[side, c],
+            near_recv.at[side, c],
+            device,
+        )
+        for c in range(chunks)
+        for side, device, there in ((0, to_up, up), (1, to_down, down))
+    ]
+    sums = [
+        remote(
+            summed.at[side, rows(c * CHUNK)],
+            arrived.at[rows(side * half + c * CHUNK)],
+            summed_send.at[side, c],
+            summed_recv.at[side, c],
+            device,
+        )
+        for c in range(chunks)
+        for side, device in ((0, to_down), (1, to_up))
+    ]
+
     for copy in small_loads:
         copy.wait()
     own_load.wait()
-    prepare(0, half)
-    for c in range(early):
+    for c in range(all_chunks):
+        prepare(c * CHUNK, CHUNK)
         halo_sent(c)
-
-    raw = []
-    for c in range(chunks):
-        for side, device in ((0, to_down), (1, to_up)):
-            copy = remote(
-                ints.at[rows(far * pairs + side * half + c * CHUNK)],
-                via.at[side, rows(c * CHUNK), pl.ds(depth, depth)],
-                raw_send.at[side, c],
-                raw_recv.at[side, c],
-                device,
-            )
-            copy.start()
-            raw.append(copy)
-
-    prepare(half, pairs - half)
-    for c in range(early, all_chunks):
-        halo_sent(c)
-
-    for copy in via_loads:
-        copy.wait()
-    near, sums = [], []
-    for c in range(chunks):
-        for side, device, there in ((0, to_up, up), (1, to_down, down)):
-            copy = remote(
-                ints.at[rows(there * pairs + side * half + c * CHUNK)],
-                own.at[rows(side * half + c * CHUNK), pl.ds(depth, depth)],
-                near_send.at[side, c],
-                near_recv.at[side, c],
-                device,
-            )
-            copy.start()
-            near.append(copy)
-        for side, device in ((0, to_down), (1, to_up)):
-            raw[c * 2 + side].wait_recv()
-            for p in range(c * CHUNK, c * CHUNK + CHUNK):
-                block = via[side, p]
-                summed[side, p] = contract(block[:, :width], block[:, width:], 0, 0).astype(BF16)
-            copy = remote(
-                summed.at[side, rows(c * CHUNK)],
-                arrived.at[rows(side * half + c * CHUNK)],
-                summed_send.at[side, c],
-                summed_recv.at[side, c],
-                device,
-            )
-            copy.start()
-            sums.append(copy)
+        if c + early < all_chunks:
+            send_halo(c + early)
+        if c == all_chunks - 2:
+            for copy in raw:
+                copy.start()
 
     for part, none in ((0, no_left), (2, no_right)):
 
@@ -303,7 +300,25 @@
             acc[p] += contract(flipped[p], right_half, 1, 0)
         return carry
 
-    lax.fori_loop(0, pairs // TOGETHER, couple, 0)
+    steps = pairs // TOGETHER
+    lax.fori_loop(0, steps // 4, couple, 0)
+    for copy in raw[:2]:
+        copy.wait_send()
+    for copy in near:
+        copy.start()
+    lax.fori_loop(steps // 4, steps // 2, couple, 0)
+
+    for copy in via_loads:
+        copy.wait()
+    for c in range(chunks):
+        for side in (0, 1):
+            raw[c * 2 + side].wait_recv()
+            for p in range(c * CHUNK, c * CHUNK + CHUNK):
+                block = via[side, p]
+                summed[side, p] = contract(block[:, :width], block[:, width:], 0, 0).astype(BF16)
+            sums[c * 2 + side].start()
+
+    lax.fori_loop(steps // 2, steps, couple, 0)
 
     for c in range(chunks):
         for side in (0, 1):
@@ -317,7 +332,7 @@
                 residual[p] = result
                 updated[p] = (amps[p].astype(F32) - result * inverse[p]).astype(BF16)
 
-    for copy in raw + near + sums + domain_halo:
+    for copy in raw[2:] + near + sums + domain_halo:
         copy.wait_send()
 
     @pl.when(passes)

time: 38.7 us -> 41.9 us (1.083)
  the two profiles are of different devices: /device:TPU:6 before, /device:TPU:1 now
where the time goes in v5:
time: 41.9 us; the launch traced here: 41.7 us
  Pallas kernels  39.3 us (94%)
  local copies, waits for them, and re-layouts  1.77 us (4%)
  between operations  0.64 us (2%)
    pallas_call x1, Pallas kernels, per_device(): pl.pallas_call(kernel, out_shape=(pltpu.VMEM((pairs, width, width), F32),...  39.3 us
    unnamed x2, local copies, waits for them, and re-layouts  1.77 us

profile of v5, /device:TPU:1, one launch (start us, length us, event | category | flops | bytes accessed | tf_op | source)
XLA Modules:
  0.0 41.7 jit_solution(16912298989428473573)
XLA Ops:
  0.6 39.3 %doubles_residual.1 = (f32[16,128,128]{2,1,0:T(8,128)S(1)}, bf16[16,128,128]{2,1,0:T(8,128)(2,1)S(1)}) custom-call(bf16[64,64,256]{2,1,0:T(8,128)(2,1)} %ints.1, bf16[16,128,128]{2,1,0:T(8,128)(2,1)} %amps_in.1, bf16[16,128,128]{2,1,0:T(8,128)(2,1)} %coeffs_in.1, s32[16,128]{1,0:T(8,128)} %domains_in.1, s32[8,16]{1,0:T(8,128)} %bitcast.2, s32[16]{0:T(128)} %counts_in.1, ...), custom_call_target="tpu_custom_call" | custom-call | tf_op jit(solution)/shard_map/doubles_residual/pallas_call | solution.py:365
  40.0 1.0 %copy.13 = f32[16,128,128]{2,1,0:T(8,128)} copy(f32[16,128,128]{2,1,0:T(8,128)S(1)} %get-tuple-element.2) | data formatting | bytes 2097152
  40.9 0.8 %copy.14 = bf16[16,128,128]{2,1,0:T(8,128)(2,1)} copy(bf16[16,128,128]{2,1,0:T(8,128)(2,1)S(1)} %get-tuple-element.3) | data formatting | bytes 1048576

commit v6 on v5

--- a/solution.py
+++ b/solution.py
@@ -102,9 +102,7 @@
         for p, block in zip(here, left_half):
             pao[pairs + p] = contract(block, coeffs[p], 1, 1).astype(BF16)
 
-    early = all_chunks // 2
-    for c in range(early):
-        to_pao(c)
+    to_pao(0)
     domain_load.wait()
 
     pl.semaphore_wait(barrier, jnp.where(at_end, 3, 2))
@@ -112,6 +110,20 @@
     @pl.when(jnp.logical_and(last_end, pair < n_pair - 1))
     def _():
         greet(ready, next_pair)
+
+    raw = [
+        remote(
+            ints.at[rows(far * pairs + side * half + c * CHUNK)],
+            via.at[side, rows(c * CHUNK), pl.ds(depth, depth)],
+            raw_send.at[side, c],
+            raw_recv.at[side, c],
+            device,
+        )
+        for c in range(chunks)
+        for side, device in ((0, to_down), (1, to_up))
+    ]
+    for copy in raw:
+        copy.start()
 
     targets = (
         (0, to_up, jnp.where(last_end, 3, 0)),
@@ -143,14 +155,11 @@
         for c in range(all_chunks)
     ]
 
-    def send_halo(c):
+    for c in range(all_chunks):
+        if c > 0:
+            to_pao(c)
         for copy in halo[c]:
             copy.start()
-
-    for c in range(early):
-        send_halo(c)
-    for c in range(early, all_chunks):
-        to_pao(c)
 
     def arrival(part, c):
         return remote(
@@ -186,27 +195,28 @@
         for c in range(all_chunks)
     ]
 
-    def halo_sent(c):
-        for copy in halo[c]:
-            copy.wait_send()
-
+    def pass_on():
         @pl.when(at_end)
         def _():
-            if c == 0:
-                domain_arrival(3).wait_recv()
-            arrival(3, c).wait_recv()
-
-        if c == 0:
-
-            @pl.when(jnp.logical_and(last_end, pair > 0))
-            def _():
-                pl.semaphore_wait(ready, 1)
+            domain_arrival(3).wait_recv()
+
+        @pl.when(jnp.logical_and(last_end, pair > 0))
+        def _():
+            pl.semaphore_wait(ready, 1)
 
         @pl.when(passes)
         def _():
-            if c == 0:
-                domain_pass.start()
-            passed[c].start()
+            domain_pass.start()
+
+        for c in range(all_chunks):
+
+            @pl.when(at_end)
+            def _():
+                arrival(3, c).wait_recv()
+
+            @pl.when(passes)
+            def _():
+                passed[c].start()
 
     def prepare(first, count):
         for p in range(first, first + count):
@@ -219,17 +229,6 @@
             mine[p] = jnp.broadcast_to(doms[pl.ds(pairs + p, 1), :], (width, width)).T
             flipped[p] = coeffs[p].T
 
-    raw = [
-        remote(
-            ints.at[rows(far * pairs + side * half + c * CHUNK)],
-            via.at[side, rows(c * CHUNK), pl.ds(depth, depth)],
-            raw_send.at[side, c],
-            raw_recv.at[side, c],
-            device,
-        )
-        for c in range(chunks)
-        for side, device in ((0, to_down), (1, to_up))
-    ]
     near = [
         remote(
             ints.at[rows(there * pairs + side * half + c * CHUNK)],
@@ -256,14 +255,22 @@
     for copy in small_loads:
         copy.wait()
     own_load.wait()
-    for c in range(all_chunks):
-        prepare(c * CHUNK, CHUNK)
-        halo_sent(c)
-        if c + early < all_chunks:
-            send_halo(c + early)
-        if c == all_chunks - 2:
-            for copy in raw:
-                copy.start()
+    prepare(0, half)
+
+    for copy in via_loads:
+        copy.wait()
+    for c in range(chunks):
+        for side in (0, 1):
+            raw[c * 2 + side].wait_recv()
+            for p in range(c * CHUNK, c * CHUNK + CHUNK):
+                block = via[side, p]
+                summed[side, p] = contract(block[:, :width], block[:, width:], 0, 0).astype(BF16)
+            sums[c * 2 + side].start()
+    for copy in near:
+        copy.start()
+
+    prepare(half, pairs - half)
+    pass_on()
 
     for part, none in ((0, no_left), (2, no_right)):
 
@@ -300,25 +307,7 @@
             acc[p] += contract(flipped[p], right_half, 1, 0)
         return carry
 
-    steps = pairs // TOGETHER
-    lax.fori_loop(0, steps // 4, couple, 0)
-    for copy in raw[:2]:
-        copy.wait_send()
-    for copy in near:
-        copy.start()
-    lax.fori_loop(steps // 4, steps // 2, couple, 0)
-
-    for copy in via_loads:
-        copy.wait()
-    for c in range(chunks):
-        for side in (0, 1):
-            raw[c * 2 + side].wait_recv()
-            for p in range(c * CHUNK, c * CHUNK + CHUNK):
-                block = via[side, p]
-                summed[side, p] = contract(block[:, :width], block[:, width:], 0, 0).astype(BF16)
-            sums[c * 2 + side].start()
-
-    lax.fori_loop(steps // 2, steps, couple, 0)
+    lax.fori_loop(0, pairs // TOGETHER, couple, 0)
 
     for c in range(chunks):
         for side in (0, 1):
@@ -332,13 +321,24 @@
                 residual[p] = result
                 updated[p] = (amps[p].astype(F32) - result * inverse[p]).astype(BF16)
 
-    for copy in raw[2:] + near + sums + domain_halo:
+    for copy in raw + near + sums + domain_halo + sum(halo, []):
         copy.wait_send()
 
     @pl.when(passes)
     def _():
         for copy in [domain_pass] + passed:
             copy.wait_send()
+
+
+def hand_over(residual_in, updated_in, residual, updated, sems):
+    copies = [
+        pltpu.make_async_copy(residual_in, residual, sems.at[0]),
+        pltpu.make_async_copy(updated_in, updated, sems.at[1]),
+    ]
+    for copy in copies:
+        copy.start()
+    for copy in copies:
+        copy.wait()
 
 
 def per_device(
@@ -412,7 +412,18 @@
         ),
         name="doubles_residual",
     )(*(pltpu.with_memory_space_constraint(operand, pltpu.HBM) for operand in operands))
-    return (residual, updated)
+    return pl.pallas_call(
+        hand_over,
+        out_shape=(
+            jax.ShapeDtypeStruct((pairs, width, width), F32),
+            jax.ShapeDtypeStruct((pairs, width, width), BF16),
+        ),
+        in_specs=(in_vmem, in_vmem),
+        out_specs=(in_hbm, in_hbm),
+        scratch_shapes=[dma((2,))],
+        compiler_params=pltpu.CompilerParams(vmem_limit_bytes=16 * 1024 * 1024),
+        name="hand_over",
+    )(residual, updated)
 
 
 def solution(mesh):

time: 41.9 us -> 42.2 us (level)
  the two profiles are of different devices: /device:TPU:1 before, /device:TPU:6 now
where the time goes in v6:
time: 42.2 us; the launch traced here: 42.1 us
  Pallas kernels  41.4 us (98%)
  between operations  0.64 us (2%)
    pallas_call x1, Pallas kernels, per_device(): pl.pallas_call(kernel, out_shape=(pltpu.VMEM((pairs, width, width), F32),...  40.3 us
    pallas_call x1, Pallas kernels, per_device(): pl.pallas_call(hand_over, out_shape=(jax.ShapeDtypeStruct((pairs, width,...  1.16 us

profile of v6, /device:TPU:6, one launch (start us, length us, event | category | flops | bytes accessed | tf_op | source)
XLA Modules:
  0.0 42.1 jit_solution(9114964558491616983)
XLA Ops:
  0.6 40.3 %doubles_residual.1 = (f32[16,128,128]{2,1,0:T(8,128)S(1)}, bf16[16,128,128]{2,1,0:T(8,128)(2,1)S(1)}) custom-call(bf16[64,64,256]{2,1,0:T(8,128)(2,1)} %ints.1, bf16[16,128,128]{2,1,0:T(8,128)(2,1)} %amps_in.1, bf16[16,128,128]{2,1,0:T(8,128)(2,1)} %coeffs_in.1, s32[16,128]{1,0:T(8,128)} %domains_in.1, s32[8,16]{1,0:T(8,128)} %bitcast.2, s32[16]{0:T(128)} %counts_in.1, ...), custom_call_target="tpu_custom_call" | custom-call | tf_op jit(solution)/shard_map/doubles_residual/pallas_call | solution.py:365
  40.9 1.2 %hand_over.1 = (f32[16,128,128]{2,1,0:T(8,128)}, bf16[16,128,128]{2,1,0:T(8,128)(2,1)}) custom-call(f32[16,128,128]{2,1,0:T(8,128)S(1)} %get-tuple-element.4.residual_in, bf16[16,128,128]{2,1,0:T(8,128)(2,1)S(1)} %get-tuple-element.5.updated_in), custom_call_target="tpu_custom_call" | custom-call | tf_op jit(solution)/shard_map/hand_over/pallas_call | solution.py:415

commit v7 on v6

--- a/solution.py
+++ b/solution.py
@@ -104,6 +104,7 @@
 
     to_pao(0)
     domain_load.wait()
+    early = all_chunks // 2
 
     pl.semaphore_wait(barrier, jnp.where(at_end, 3, 2))
 
@@ -122,9 +123,6 @@
         for c in range(chunks)
         for side, device in ((0, to_down), (1, to_up))
     ]
-    for copy in raw:
-        copy.start()
-
     targets = (
         (0, to_up, jnp.where(last_end, 3, 0)),
         (1, to_down, jnp.where(first_end, 3, 2)),
@@ -158,8 +156,9 @@
     for c in range(all_chunks):
         if c > 0:
             to_pao(c)
-        for copy in halo[c]:
-            copy.start()
+        if c < early:
+            for copy in halo[c]:
+                copy.start()
 
     def arrival(part, c):
         return remote(
@@ -195,28 +194,31 @@
         for c in range(all_chunks)
     ]
 
-    def pass_on():
+    def halo_sent(c):
+        for copy in halo[c]:
+            copy.wait_send()
+        if c + early < all_chunks:
+            for copy in halo[c + early]:
+                copy.start()
+
+    def pass_on(c):
         @pl.when(at_end)
         def _():
-            domain_arrival(3).wait_recv()
-
-        @pl.when(jnp.logical_and(last_end, pair > 0))
-        def _():
-            pl.semaphore_wait(ready, 1)
+            if c == 0:
+                domain_arrival(3).wait_recv()
+            arrival(3, c).wait_recv()
+
+        if c == 0:
+
+            @pl.when(jnp.logical_and(last_end, pair > 0))
+            def _():
+                pl.semaphore_wait(ready, 1)
 
         @pl.when(passes)
         def _():
-            domain_pass.start()
-
-        for c in range(all_chunks):
-
-            @pl.when(at_end)
-            def _():
-                arrival(3, c).wait_recv()
-
-            @pl.when(passes)
-            def _():
-                passed[c].start()
+            if c == 0:
+                domain_pass.start()
+            passed[c].start()
 
     def prepare(first, count):
         for p in range(first, first + count):
@@ -255,7 +257,16 @@
     for copy in small_loads:
         copy.wait()
     own_load.wait()
-    prepare(0, half)
+    for c in range(all_chunks):
+        prepare(c * CHUNK, CHUNK)
+        halo_sent(c)
+        if c == early - 1:
+            for copy in raw:
+                copy.start()
+        if c >= early:
+            for copy in near[(c - early) * 2 : (c - early) * 2 + 2]:
+                copy.start()
+        pass_on(c)
 
     for copy in via_loads:
         copy.wait()
@@ -266,11 +277,6 @@
                 block = via[side, p]
                 summed[side, p] = contract(block[:, :width], block[:, width:], 0, 0).astype(BF16)
             sums[c * 2 + side].start()
-    for copy in near:
-        copy.start()
-
-    prepare(half, pairs - half)
-    pass_on()
 
     for part, none in ((0, no_left), (2, no_right)):
 
@@ -321,7 +327,7 @@
                 residual[p] = result
                 updated[p] = (amps[p].astype(F32) - result * inverse[p]).astype(BF16)
 
-    for copy in raw + near + sums + domain_halo + sum(halo, []):
+    for copy in raw + near + sums + domain_halo:
         copy.wait_send()
 
     @pl.when(passes)

time: 42.2 us -> 38 us (0.900)
  Pallas kernels: 41.4 us -> 37 us
    pallas_call x1, Pallas kernels: 40.3 us -> 35.8 us  [per_device(): pl.pallas_call(kernel, out_shape=(pltpu.VMEM((pairs, width, width), F32),...]
where the time goes in v7:
time: 38 us; the launch traced here: 37.6 us
  Pallas kernels  37 us (97%)
  between operations  0.64 us (2%)
    pallas_call x1, Pallas kernels, per_device(): pl.pallas_call(kernel, out_shape=(pltpu.VMEM((pairs, width, width), F32),...  35.8 us
    pallas_call x1, Pallas kernels, per_device(): pl.pallas_call(hand_over, out_shape=(jax.ShapeDtypeStruct((pairs, width,...  1.16 us

profile of v7, /device:TPU:6, one launch (start us, length us, event | category | flops | bytes accessed | tf_op | source)
XLA Modules:
  0.0 37.6 jit_solution(3254962577118239067)
XLA Ops:
  0.6 35.8 %doubles_residual.1 = (f32[16,128,128]{2,1,0:T(8,128)S(1)}, bf16[16,128,128]{2,1,0:T(8,128)(2,1)S(1)}) custom-call(bf16[64,64,256]{2,1,0:T(8,128)(2,1)} %ints.1, bf16[16,128,128]{2,1,0:T(8,128)(2,1)} %amps_in.1, bf16[16,128,128]{2,1,0:T(8,128)(2,1)} %coeffs_in.1, s32[16,128]{1,0:T(8,128)} %domains_in.1, s32[8,16]{1,0:T(8,128)} %bitcast.2, s32[16]{0:T(128)} %counts_in.1, ...), custom_call_target="tpu_custom_call" | custom-call | tf_op jit(solution)/shard_map/doubles_residual/pallas_call | solution.py:371
  36.5 1.2 %hand_over.1 = (f32[16,128,128]{2,1,0:T(8,128)}, bf16[16,128,128]{2,1,0:T(8,128)(2,1)}) custom-call(f32[16,128,128]{2,1,0:T(8,128)S(1)} %get-tuple-element.4.residual_in, bf16[16,128,128]{2,1,0:T(8,128)(2,1)S(1)} %get-tuple-element.5.updated_in), custom_call_target="tpu_custom_call" | custom-call | tf_op jit(solution)/shard_map/hand_over/pallas_call | solution.py:421

commit v8 on v7

--- a/solution.py
+++ b/solution.py
@@ -156,9 +156,8 @@
     for c in range(all_chunks):
         if c > 0:
             to_pao(c)
-        if c < early:
-            for copy in halo[c]:
-                copy.start()
+        for copy in halo[c]:
+            copy.start()
 
     def arrival(part, c):
         return remote(
@@ -197,9 +196,6 @@
     def halo_sent(c):
         for copy in halo[c]:
             copy.wait_send()
-        if c + early < all_chunks:
-            for copy in halo[c + early]:
-                copy.start()
 
     def pass_on(c):
         @pl.when(at_end)
@@ -267,16 +263,6 @@
             for copy in near[(c - early) * 2 : (c - early) * 2 + 2]:
                 copy.start()
         pass_on(c)
-
-    for copy in via_loads:
-        copy.wait()
-    for c in range(chunks):
-        for side in (0, 1):
-            raw[c * 2 + side].wait_recv()
-            for p in range(c * CHUNK, c * CHUNK + CHUNK):
-                block = via[side, p]
-                summed[side, p] = contract(block[:, :width], block[:, width:], 0, 0).astype(BF16)
-            sums[c * 2 + side].start()
 
     for part, none in ((0, no_left), (2, no_right)):
 
@@ -313,7 +299,20 @@
             acc[p] += contract(flipped[p], right_half, 1, 0)
         return carry
 
-    lax.fori_loop(0, pairs // TOGETHER, couple, 0)
+    steps = pairs // TOGETHER
+    lax.fori_loop(0, steps // 2, couple, 0)
+
+    for copy in via_loads:
+        copy.wait()
+    for c in range(chunks):
+        for side in (0, 1):
+            raw[c * 2 + side].wait_recv()
+            for p in range(c * CHUNK, c * CHUNK + CHUNK):
+                block = via[side, p]
+                summed[side, p] = contract(block[:, :width], block[:, width:], 0, 0).astype(BF16)
+            sums[c * 2 + side].start()
+
+    lax.fori_loop(steps // 2, steps, couple, 0)
 
     for c in range(chunks):
         for side in (0, 1):

time: 38 us -> 38.7 us (1.018)
  the two profiles are of different devices: /device:TPU:6 before, /device:TPU:14 now
where the time goes in v8:
time: 38.7 us; the launch traced here: 38.6 us
  Pallas kernels  38 us (98%)
  between operations  0.64 us (2%)
    pallas_call x1, Pallas kernels, per_device(): pl.pallas_call(kernel, out_shape=(pltpu.VMEM((pairs, width, width), F32),...  36.8 us
    pallas_call x1, Pallas kernels, per_device(): pl.pallas_call(hand_over, out_shape=(jax.ShapeDtypeStruct((pairs, width,...  1.16 us

profile of v8, /device:TPU:14, one launch (start us, length us, event | category | flops | bytes accessed | tf_op | source)
XLA Modules:
  0.0 38.6 jit_solution(1918288640831912892)
XLA Ops:
  0.6 36.8 %doubles_residual.1 = (f32[16,128,128]{2,1,0:T(8,128)S(1)}, bf16[16,128,128]{2,1,0:T(8,128)(2,1)S(1)}) custom-call(bf16[64,64,256]{2,1,0:T(8,128)(2,1)} %ints.1, bf16[16,128,128]{2,1,0:T(8,128)(2,1)} %amps_in.1, bf16[16,128,128]{2,1,0:T(8,128)(2,1)} %coeffs_in.1, s32[16,128]{1,0:T(8,128)} %domains_in.1, s32[8,16]{1,0:T(8,128)} %bitcast.2, s32[16]{0:T(128)} %counts_in.1, ...), custom_call_target="tpu_custom_call" | custom-call | tf_op jit(solution)/shard_map/doubles_residual/pallas_call | solution.py:370
  37.4 1.2 %hand_over.1 = (f32[16,128,128]{2,1,0:T(8,128)}, bf16[16,128,128]{2,1,0:T(8,128)(2,1)}) custom-call(f32[16,128,128]{2,1,0:T(8,128)S(1)} %get-tuple-element.4.residual_in, bf16[16,128,128]{2,1,0:T(8,128)(2,1)S(1)} %get-tuple-element.5.updated_in), custom_call_target="tpu_custom_call" | custom-call | tf_op jit(solution)/shard_map/hand_over/pallas_call | solution.py:420

commit v9 on v7

--- a/solution.py
+++ b/solution.py
@@ -102,8 +102,6 @@
         for p, block in zip(here, left_half):
             pao[pairs + p] = contract(block, coeffs[p], 1, 1).astype(BF16)
 
-    to_pao(0)
-    domain_load.wait()
     early = all_chunks // 2
 
     pl.semaphore_wait(barrier, jnp.where(at_end, 3, 2))
@@ -123,6 +121,20 @@
         for c in range(chunks)
         for side, device in ((0, to_down), (1, to_up))
     ]
+    near = [
+        remote(
+            ints.at[rows(there * pairs + side * half + c * CHUNK)],
+            own.at[rows(side * half + c * CHUNK), pl.ds(depth, depth)],
+            near_send.at[side, c],
+            near_recv.at[side, c],
+            device,
+        )
+        for c in range(chunks)
+        for side, device, there in ((0, to_up, up), (1, to_down, down))
+    ]
+    for copy in near[:2]:
+        copy.start()
+
     targets = (
         (0, to_up, jnp.where(last_end, 3, 0)),
         (1, to_down, jnp.where(first_end, 3, 2)),
@@ -137,6 +149,7 @@
         )
         for side, device, part in targets
     ]
+    domain_load.wait()
     for copy in domain_halo:
         copy.start()
     halo = [
@@ -154,11 +167,9 @@
     ]
 
     for c in range(all_chunks):
-        if c > 0:
-            to_pao(c)
-        if c < early:
-            for copy in halo[c]:
-                copy.start()
+        to_pao(c)
+        for copy in halo[c]:
+            copy.start()
 
     def arrival(part, c):
         return remote(
@@ -197,9 +208,6 @@
     def halo_sent(c):
         for copy in halo[c]:
             copy.wait_send()
-        if c + early < all_chunks:
-            for copy in halo[c + early]:
-                copy.start()
 
     def pass_on(c):
         @pl.when(at_end)
@@ -231,17 +239,6 @@
             mine[p] = jnp.broadcast_to(doms[pl.ds(pairs + p, 1), :], (width, width)).T
             flipped[p] = coeffs[p].T
 
-    near = [
-        remote(
-            ints.at[rows(there * pairs + side * half + c * CHUNK)],
-            own.at[rows(side * half + c * CHUNK), pl.ds(depth, depth)],
-            near_send.at[side, c],
-            near_recv.at[side, c],
-            device,
-        )
-        for c in range(chunks)
-        for side, device, there in ((0, to_up, up), (1, to_down, down))
-    ]
     sums = [
         remote(
             summed.at[side, rows(c * CHUNK)],
@@ -263,8 +260,8 @@
         if c == early - 1:
             for copy in raw:
                 copy.start()
-        if c >= early:
-            for copy in near[(c - early) * 2 : (c - early) * 2 + 2]:
+        if c == early:
+            for copy in near[2:]:
                 copy.start()
         pass_on(c)
 
@@ -318,12 +315,16 @@
     for c in range(chunks):
         for side in (0, 1):
             near[c * 2 + side].wait_recv()
+            first = side * half + c * CHUNK
+            for p in range(first, first + CHUNK):
+                block = own[p, pl.ds(depth, depth), :]
+                acc[p] += contract(block[:, :width], block[:, width:], 0, 0)
+    for c in range(chunks):
+        for side in (0, 1):
             sums[c * 2 + side].wait_recv()
             first = side * half + c * CHUNK
             for p in range(first, first + CHUNK):
-                block = own[p, pl.ds(depth, depth), :]
-                exchange = contract(block[:, :width], block[:, width:], 0, 0) + arrived[p].astype(F32)
-                result = acc[p] + exchange
+                result = acc[p] + arrived[p].astype(F32)
                 residual[p] = result
                 updated[p] = (amps[p].astype(F32) - result * inverse[p]).astype(BF16)
 

time: 38 us -> 38.4 us (1.011)
  Pallas kernels: 37 us -> 37.6 us
    pallas_call x1, Pallas kernels: 35.8 us -> 36.4 us  [per_device(): pl.pallas_call(kernel, out_shape=(pltpu.VMEM((pairs, width, width), F32),...]
where the time goes in v9:
time: 38.4 us; the launch traced here: 38.2 us
  Pallas kernels  37.6 us (98%)
  between operations  0.64 us (2%)
    pallas_call x1, Pallas kernels, per_device(): pl.pallas_call(kernel, out_shape=(pltpu.VMEM((pairs, width, width), F32),...  36.4 us
    pallas_call x1, Pallas kernels, per_device(): pl.pallas_call(hand_over, out_shape=(jax.ShapeDtypeStruct((pairs, width,...  1.16 us

profile of v9, /device:TPU:6, one launch (start us, length us, event | category | flops | bytes accessed | tf_op | source)
XLA Modules:
  0.0 38.2 jit_solution(13280868920051993170)
XLA Ops:
  0.6 36.4 %doubles_residual.1 = (f32[16,128,128]{2,1,0:T(8,128)S(1)}, bf16[16,128,128]{2,1,0:T(8,128)(2,1)S(1)}) custom-call(bf16[64,64,256]{2,1,0:T(8,128)(2,1)} %ints.1, bf16[16,128,128]{2,1,0:T(8,128)(2,1)} %amps_in.1, bf16[16,128,128]{2,1,0:T(8,128)(2,1)} %coeffs_in.1, s32[16,128]{1,0:T(8,128)} %domains_in.1, s32[8,16]{1,0:T(8,128)} %bitcast.2, s32[16]{0:T(128)} %counts_in.1, ...), custom_call_target="tpu_custom_call" | custom-call | tf_op jit(solution)/shard_map/doubles_residual/pallas_call | solution.py:372
  37.1 1.2 %hand_over.1 = (f32[16,128,128]{2,1,0:T(8,128)}, bf16[16,128,128]{2,1,0:T(8,128)(2,1)}) custom-call(f32[16,128,128]{2,1,0:T(8,128)S(1)} %get-tuple-element.4.residual_in, bf16[16,128,128]{2,1,0:T(8,128)(2,1)S(1)} %get-tuple-element.5.updated_in), custom_call_target="tpu_custom_call" | custom-call | tf_op jit(solution)/shard_map/hand_over/pallas_call | solution.py:422

commit v10 on v9

--- a/solution.py
+++ b/solution.py
@@ -9,7 +9,7 @@
 F32 = jnp.float32
 BF16 = jnp.bfloat16
 CHUNK = 4
-TOGETHER = 4
+TOGETHER = 8
 
 
 def contract(a, b, dim_a, dim_b):
@@ -257,7 +257,7 @@
     for c in range(all_chunks):
         prepare(c * CHUNK, CHUNK)
         halo_sent(c)
-        if c == early - 1:
+        if c == 0:
             for copy in raw:
                 copy.start()
         if c == early:
@@ -274,6 +274,16 @@
                 block = via[side, p]
                 summed[side, p] = contract(block[:, :width], block[:, width:], 0, 0).astype(BF16)
             sums[c * 2 + side].start()
+
+    def add_near(c):
+        for side in (0, 1):
+            near[c * 2 + side].wait_recv()
+            first = side * half + c * CHUNK
+            for p in range(first, first + CHUNK):
+                block = own[p, pl.ds(depth, depth), :]
+                acc[p] += contract(block[:, :width], block[:, width:], 0, 0)
+
+    add_near(0)
 
     for part, none in ((0, no_left), (2, no_right)):
 
@@ -312,13 +322,8 @@
 
     lax.fori_loop(0, pairs // TOGETHER, couple, 0)
 
-    for c in range(chunks):
-        for side in (0, 1):
-            near[c * 2 + side].wait_recv()
-            first = side * half + c * CHUNK
-            for p in range(first, first + CHUNK):
-                block = own[p, pl.ds(depth, depth), :]
-                acc[p] += contract(block[:, :width], block[:, width:], 0, 0)
+    for c in range(1, chunks):
+        add_near(c)
     for c in range(chunks):
         for side in (0, 1):
             sums[c * 2 + side].wait_recv()

time: 38.4 us -> 37.2 us (0.969)
  Pallas kernels: 37.6 us -> 36.1 us
    pallas_call x1, Pallas kernels: 36.4 us -> 34.9 us  [per_device(): pl.pallas_call(kernel, out_shape=(pltpu.VMEM((pairs, width, width), F32),...]
where the time goes in v10:
time: 37.2 us; the launch traced here: 36.7 us
  Pallas kernels  36.1 us (97%)
  between operations  0.64 us (2%)
    pallas_call x1, Pallas kernels, per_device(): pl.pallas_call(kernel, out_shape=(pltpu.VMEM((pairs, width, width), F32),...  34.9 us
    pallas_call x1, Pallas kernels, per_device(): pl.pallas_call(hand_over, out_shape=(jax.ShapeDtypeStruct((pairs, width,...  1.16 us

profile of v10, /device:TPU:6, one launch (start us, length us, event | category | flops | bytes accessed | tf_op | source)
XLA Modules:
  0.0 36.7 jit_solution(17732729931453383986)
XLA Ops:
  0.6 34.9 %doubles_residual.1 = (f32[16,128,128]{2,1,0:T(8,128)S(1)}, bf16[16,128,128]{2,1,0:T(8,128)(2,1)S(1)}) custom-call(bf16[64,64,256]{2,1,0:T(8,128)(2,1)} %ints.1, bf16[16,128,128]{2,1,0:T(8,128)(2,1)} %amps_in.1, bf16[16,128,128]{2,1,0:T(8,128)(2,1)} %coeffs_in.1, s32[16,128]{1,0:T(8,128)} %domains_in.1, s32[8,16]{1,0:T(8,128)} %bitcast.2, s32[16]{0:T(128)} %counts_in.1, ...), custom_call_target="tpu_custom_call" | custom-call | tf_op jit(solution)/shard_map/doubles_residual/pallas_call | solution.py:377
  35.6 1.2 %hand_over.1 = (f32[16,128,128]{2,1,0:T(8,128)}, bf16[16,128,128]{2,1,0:T(8,128)(2,1)}) custom-call(f32[16,128,128]{2,1,0:T(8,128)S(1)} %get-tuple-element.4.residual_in, bf16[16,128,128]{2,1,0:T(8,128)(2,1)S(1)} %get-tuple-element.5.updated_in), custom_call_target="tpu_custom_call" | custom-call | tf_op jit(solution)/shard_map/hand_over/pallas_call | solution.py:427

commit v11 on v10

--- a/solution.py
+++ b/solution.py
@@ -8,7 +8,7 @@
 MESH = pl.DeviceIdType.MESH
 F32 = jnp.float32
 BF16 = jnp.bfloat16
-CHUNK = 4
+CHUNK = 2
 TOGETHER = 8
 
 

time: 37.2 us -> 37.7 us (1.013)
  no operation moved by 1% of the time
where the time goes in v11:
time: 37.7 us; the launch traced here: 37 us
  Pallas kernels  36.4 us (97%)
  between operations  0.64 us (2%)
    pallas_call x1, Pallas kernels, per_device(): pl.pallas_call(kernel, out_shape=(pltpu.VMEM((pairs, width, width), F32),...  35.2 us
    pallas_call x1, Pallas kernels, per_device(): pl.pallas_call(hand_over, out_shape=(jax.ShapeDtypeStruct((pairs, width,...  1.16 us

profile of v11, /device:TPU:6, one launch (start us, length us, event | category | flops | bytes accessed | tf_op | source)
XLA Modules:
  0.0 37.0 jit_solution(3535271189148494568)
XLA Ops:
  0.6 35.2 %doubles_residual.1 = (f32[16,128,128]{2,1,0:T(8,128)S(1)}, bf16[16,128,128]{2,1,0:T(8,128)(2,1)S(1)}) custom-call(bf16[64,64,256]{2,1,0:T(8,128)(2,1)} %ints.1, bf16[16,128,128]{2,1,0:T(8,128)(2,1)} %amps_in.1, bf16[16,128,128]{2,1,0:T(8,128)(2,1)} %coeffs_in.1, s32[16,128]{1,0:T(8,128)} %domains_in.1, s32[8,16]{1,0:T(8,128)} %bitcast.2, s32[16]{0:T(128)} %counts_in.1, ...), custom_call_target="tpu_custom_call" | custom-call | tf_op jit(solution)/shard_map/doubles_residual/pallas_call | solution.py:377
  35.9 1.2 %hand_over.1 = (f32[16,128,128]{2,1,0:T(8,128)}, bf16[16,128,128]{2,1,0:T(8,128)(2,1)}) custom-call(f32[16,128,128]{2,1,0:T(8,128)S(1)} %get-tuple-element.4.residual_in, bf16[16,128,128]{2,1,0:T(8,128)(2,1)S(1)} %get-tuple-element.5.updated_in), custom_call_target="tpu_custom_call" | custom-call | tf_op jit(solution)/shard_map/hand_over/pallas_call | solution.py:427

commit v12 on v10

--- a/solution.py
+++ b/solution.py
@@ -112,13 +112,12 @@
 
     raw = [
         remote(
-            ints.at[rows(far * pairs + side * half + c * CHUNK)],
-            via.at[side, rows(c * CHUNK), pl.ds(depth, depth)],
-            raw_send.at[side, c],
-            raw_recv.at[side, c],
+            ints.at[rows(far * pairs + side * half, half)],
+            via.at[side, :, pl.ds(depth, depth)],
+            raw_send.at[side],
+            raw_recv.at[side],
             device,
         )
-        for c in range(chunks)
         for side, device in ((0, to_down), (1, to_up))
     ]
     near = [
@@ -267,9 +266,10 @@
 
     for copy in via_loads:
         copy.wait()
+    for copy in raw:
+        copy.wait_recv()
     for c in range(chunks):
-        for side in (0, 1):
-            raw[c * 2 + side].wait_recv()
+        for side in (1, 0):
             for p in range(c * CHUNK, c * CHUNK + CHUNK):
                 block = via[side, p]
                 summed[side, p] = contract(block[:, :width], block[:, width:], 0, 0).astype(BF16)
@@ -405,8 +405,8 @@
             dma((6,)),
             dma(()),
             dma((2,)),
-            dma((2, chunks)),
-            dma((2, chunks)),
+            dma((2,)),
+            dma((2,)),
             dma((2, chunks)),
             dma((2, chunks)),
             dma((2, chunks)),
@@ -430,7 +430,7 @@
             jax.ShapeDtypeStruct((pairs, width, width), F32),
             jax.ShapeDtypeStruct((pairs, width, width), BF16),
         ),
-        in_specs=(in_vmem, in_vmem),
+        in_specs=(pl.BlockSpec(memory_space=pl.ANY),) * 2,
         out_specs=(in_hbm, in_hbm),
         scratch_shapes=[dma((2,))],
         compiler_params=pltpu.CompilerParams(vmem_limit_bytes=16 * 1024 * 1024),

time: 37.2 us -> 37.6 us (1.011)
  no operation moved by 1% of the time
where the time goes in v12:
time: 37.6 us; the launch traced here: 37 us
  Pallas kernels  36.4 us (97%)
  between operations  0.64 us (2%)
    pallas_call x1, Pallas kernels, per_device(): pl.pallas_call(kernel, out_shape=(pltpu.VMEM((pairs, width, width), F32),...  35.2 us
    pallas_call x1, Pallas kernels, per_device(): pl.pallas_call(hand_over, out_shape=(jax.ShapeDtypeStruct((pairs, width,...  1.16 us

profile of v12, /device:TPU:6, one launch (start us, length us, event | category | flops | bytes accessed | tf_op | source)
XLA Modules:
  0.0 37.0 jit_solution(13907883142851578371)
XLA Ops:
  0.6 35.2 %doubles_residual.1 = (f32[16,128,128]{2,1,0:T(8,128)S(1)}, bf16[16,128,128]{2,1,0:T(8,128)(2,1)S(1)}) custom-call(bf16[64,64,256]{2,1,0:T(8,128)(2,1)} %ints.1, bf16[16,128,128]{2,1,0:T(8,128)(2,1)} %amps_in.1, bf16[16,128,128]{2,1,0:T(8,128)(2,1)} %coeffs_in.1, s32[16,128]{1,0:T(8,128)} %domains_in.1, s32[8,16]{1,0:T(8,128)} %bitcast.2, s32[16]{0:T(128)} %counts_in.1, ...), custom_call_target="tpu_custom_call" | custom-call | tf_op jit(solution)/shard_map/doubles_residual/pallas_call | solution.py:377
  35.9 1.2 %hand_over.1 = (f32[16,128,128]{2,1,0:T(8,128)}, bf16[16,128,128]{2,1,0:T(8,128)(2,1)}) custom-call(f32[16,128,128]{2,1,0:T(8,128)S(1)} %get-tuple-element.4.residual_in, bf16[16,128,128]{2,1,0:T(8,128)(2,1)S(1)} %get-tuple-element.5.updated_in), custom_call_target="tpu_custom_call" | custom-call | tf_op jit(solution)/shard_map/hand_over/pallas_call | solution.py:427

commit v13 on v10

--- a/solution.py
+++ b/solution.py
@@ -268,7 +268,7 @@
     for copy in via_loads:
         copy.wait()
     for c in range(chunks):
-        for side in (0, 1):
+        for side in (1, 0):
             raw[c * 2 + side].wait_recv()
             for p in range(c * CHUNK, c * CHUNK + CHUNK):
                 block = via[side, p]
@@ -325,7 +325,7 @@
     for c in range(1, chunks):
         add_near(c)
     for c in range(chunks):
-        for side in (0, 1):
+        for side in (1, 0):
             sums[c * 2 + side].wait_recv()
             first = side * half + c * CHUNK
             for p in range(first, first + CHUNK):
@@ -430,7 +430,7 @@
             jax.ShapeDtypeStruct((pairs, width, width), F32),
             jax.ShapeDtypeStruct((pairs, width, width), BF16),
         ),
-        in_specs=(in_vmem, in_vmem),
+        in_specs=(pl.BlockSpec(memory_space=pl.ANY),) * 2,
         out_specs=(in_hbm, in_hbm),
         scratch_shapes=[dma((2,))],
         compiler_params=pltpu.CompilerParams(vmem_limit_bytes=16 * 1024 * 1024),

time: 37.2 us -> 37.3 us (level)
  no operation moved by 1% of the time
where the time goes in v13:
time: 37.3 us; the launch traced here: 36.7 us
  Pallas kernels  36.1 us (97%)
  between operations  0.64 us (2%)
    pallas_call x1, Pallas kernels, per_device(): pl.pallas_call(kernel, out_shape=(pltpu.VMEM((pairs, width, width), F32),...  34.9 us
    pallas_call x1, Pallas kernels, per_device(): pl.pallas_call(hand_over, out_shape=(jax.ShapeDtypeStruct((pairs, width,...  1.16 us

profile of v13, /device:TPU:6, one launch (start us, length us, event | category | flops | bytes accessed | tf_op | source)
XLA Modules:
  0.0 36.7 jit_solution(2268330350522153935)
XLA Ops:
  0.6 34.9 %doubles_residual.1 = (f32[16,128,128]{2,1,0:T(8,128)S(1)}, bf16[16,128,128]{2,1,0:T(8,128)(2,1)S(1)}) custom-call(bf16[64,64,256]{2,1,0:T(8,128)(2,1)} %ints.1, bf16[16,128,128]{2,1,0:T(8,128)(2,1)} %amps_in.1, bf16[16,128,128]{2,1,0:T(8,128)(2,1)} %coeffs_in.1, s32[16,128]{1,0:T(8,128)} %domains_in.1, s32[8,16]{1,0:T(8,128)} %bitcast.2, s32[16]{0:T(128)} %counts_in.1, ...), custom_call_target="tpu_custom_call" | custom-call | tf_op jit(solution)/shard_map/doubles_residual/pallas_call | solution.py:377
  35.6 1.2 %hand_over.1 = (f32[16,128,128]{2,1,0:T(8,128)}, bf16[16,128,128]{2,1,0:T(8,128)(2,1)}) custom-call(f32[16,128,128]{2,1,0:T(8,128)S(1)} %get-tuple-element.4.residual_in, bf16[16,128,128]{2,1,0:T(8,128)(2,1)S(1)} %get-tuple-element.5.updated_in), custom_call_target="tpu_custom_call" | custom-call | tf_op jit(solution)/shard_map/hand_over/pallas_call | solution.py:427

commit v14 on v12

--- a/solution.py
+++ b/solution.py
@@ -269,7 +269,7 @@
     for copy in raw:
         copy.wait_recv()
     for c in range(chunks):
-        for side in (1, 0):
+        for side in (0, 1):
             for p in range(c * CHUNK, c * CHUNK + CHUNK):
                 block = via[side, p]
                 summed[side, p] = contract(block[:, :width], block[:, width:], 0, 0).astype(BF16)

time: 37.6 us -> 37.5 us (level)
  no operation moved by 1% of the time
where the time goes in v14:
time: 37.5 us; the launch traced here: 37 us
  Pallas kernels  36.4 us (97%)
  between operations  0.64 us (2%)
    pallas_call x1, Pallas kernels, per_device(): pl.pallas_call(kernel, out_shape=(pltpu.VMEM((pairs, width, width), F32),...  35.2 us
    pallas_call x1, Pallas kernels, per_device(): pl.pallas_call(hand_over, out_shape=(jax.ShapeDtypeStruct((pairs, width,...  1.16 us

profile of v14, /device:TPU:6, one launch (start us, length us, event | category | flops | bytes accessed | tf_op | source)
XLA Modules:
  0.0 37.0 jit_solution(14565070744774606842)
XLA Ops:
  0.6 35.2 %doubles_residual.1 = (f32[16,128,128]{2,1,0:T(8,128)S(1)}, bf16[16,128,128]{2,1,0:T(8,128)(2,1)S(1)}) custom-call(bf16[64,64,256]{2,1,0:T(8,128)(2,1)} %ints.1, bf16[16,128,128]{2,1,0:T(8,128)(2,1)} %amps_in.1, bf16[16,128,128]{2,1,0:T(8,128)(2,1)} %coeffs_in.1, s32[16,128]{1,0:T(8,128)} %domains_in.1, s32[8,16]{1,0:T(8,128)} %bitcast.2, s32[16]{0:T(128)} %counts_in.1, ...), custom_call_target="tpu_custom_call" | custom-call | tf_op jit(solution)/shard_map/doubles_residual/pallas_call | solution.py:377
  35.9 1.2 %hand_over.1 = (f32[16,128,128]{2,1,0:T(8,128)}, bf16[16,128,128]{2,1,0:T(8,128)(2,1)}) custom-call(f32[16,128,128]{2,1,0:T(8,128)S(1)} %get-tuple-element.4.residual_in, bf16[16,128,128]{2,1,0:T(8,128)(2,1)S(1)} %get-tuple-element.5.updated_in), custom_call_target="tpu_custom_call" | custom-call | tf_op jit(solution)/shard_map/hand_over/pallas_call | solution.py:427
